TPU v7x, 32 devices: a whole 2x2x4 slice. The times are simulated.
32 devices in a mesh: gx: 16 (over z, x, core), gy: 2 (over y).
Axes of the slice: x: 2, y: 2, z: 4, core: 2. Of those that a mesh axis runs over, the one named last changes fastest.
Arguments:
- model_state: float32 [4, 64, 64, 256], P(None, None, 'gx', 'gy'), may hold values from -6 to 6
- density: float32 [64], replicated, may hold values from 0.3 to 1.2
- layer_in: bfloat16 [256, 256], replicated, may hold values from -0.375 to 0.375
- layer_bias: float32 [256], replicated, may hold values from -4 to 4
- layer_out: bfloat16 [256, 128], replicated, may hold values from -0.375 to 0.375
- mode_forward: float32 [64, 64], replicated, may hold values from -0.75 to 0.75
- mode_back: float32 [64, 64], replicated, may hold values from -0.75 to 0.75
- mode_rate: float32 [64], replicated, may hold values from 0.002 to 0.025
Outputs:
- new_state: float32 [4, 64, 64, 256], P(None, None, 'gx', 'gy')
All inputs are finite; a program needn't handle non-finite values.
Results may differ from a plain program's by a relative error of at most 0.0003.
Values sent between devices are 32-bit elements; how exact they have to be, the bound alone decides.
A program may use at most 64 MiB of HBM per device.

v0:
```python
import math

import jax
import jax.numpy as jnp
from jax import lax
from jax.sharding import PartitionSpec as P

HIGH = lax.Precision.HIGHEST
TIME_STEP = 0.2
BUOYANCY = 0.5


def extended(cells, sides, width):
    for axis, dim in sides:
        count = lax.axis_size(axis)
        head = lax.slice_in_dim(cells, 0, width, axis=dim)
        tail = lax.slice_in_dim(cells, cells.shape[dim] - width, cells.shape[dim], axis=dim)
        cells = jnp.concatenate(
            [
                lax.ppermute(tail, axis, [(i, (i + 1) % count) for i in range(count)]),
                cells,
                lax.ppermute(head, axis, [((i + 1) % count, i) for i in range(count)]),
            ],
            axis=dim,
        )
    return cells


def centered(values, axis_pos):
    return 0.5 * (jnp.roll(values, -1, axis_pos) - jnp.roll(values, 1, axis_pos))


def vertical(values):
    zero_layer = jnp.zeros_like(values[:1])
    upper = jnp.concatenate([values[1:], zero_layer], 0)
    lower = jnp.concatenate([zero_layer, values[:-1]], 0)
    return 0.5 * (upper - lower)


def window(values, east_offset, north_offset, margin, cells_east, cells_north):
    east_start = 2 - margin + east_offset
    north_start = 2 - margin + north_offset
    return values[
        ...,
        east_start : east_start + cells_east + 2 * margin,
        north_start : north_start + cells_north + 2 * margin,
    ]


def advect(padded, which, margin, cells_east, cells_north):
    scalar_field = padded[which]
    eastward = window(padded[0], 0, 0, margin, cells_east, cells_north)
    northward = window(padded[1], 0, 0, margin, cells_east, cells_north)
    upward = window(padded[2], 0, 0, margin, cells_east, cells_north)
    grad_east = 0.5 * (
        window(scalar_field, 1, 0, margin, cells_east, cells_north)
        - window(scalar_field, -1, 0, margin, cells_east, cells_north)
    )
    grad_north = 0.5 * (
        window(scalar_field, 0, 1, margin, cells_east, cells_north)
        - window(scalar_field, 0, -1, margin, cells_east, cells_north)
    )
    middle = window(scalar_field, 0, 0, margin, cells_east, cells_north)
    return -(eastward * grad_east + northward * grad_north + upward * vertical(middle))


def tables(length):
    positions = jnp.arange(length, dtype=jnp.int32)
    phase_angle = (positions[:, None] * positions[None, :] % length).astype(jnp.float32) * (
        2.0 * math.pi / length
    )
    return (jnp.cos(phase_angle), jnp.sin(phase_angle))


def complex_pass(cosine_table, sine_table, real_part, imag_part, formula, direction):
    common = jnp.einsum(formula, cosine_table, real_part + imag_part, precision=HIGH)
    if direction > 0:
        out_real = common + jnp.einsum(
            formula, sine_table - cosine_table, imag_part, precision=HIGH
        )
        out_imag = common - jnp.einsum(
            formula, cosine_table + sine_table, real_part, precision=HIGH
        )
    else:
        out_real = common - jnp.einsum(
            formula, cosine_table + sine_table, imag_part, precision=HIGH
        )
        out_imag = common + jnp.einsum(
            formula, sine_table - cosine_table, real_part, precision=HIGH
        )
    return (out_real, out_imag)


def rates_for(level_of, mode_rate):
    levels = mode_rate.shape[0]
    matches = level_of[None, :] == jnp.arange(levels, dtype=jnp.int32)[:, None]
    return jnp.sum(jnp.where(matches, mode_rate[:, None], 0.0), axis=0)


def on_device(
    model_state, density, layer_in, layer_bias, layer_out, mode_forward, mode_back, mode_rate
):
    fields_count, levels, cells_east, cells_north = model_state.shape
    padded = extended(model_state, (("gx", 2), ("gy", 3)), 2)
    contract_first = (((0,), (0,)), ((), ()))
    features = model_state.reshape(fields_count * levels, cells_east * cells_north).astype(
        jnp.bfloat16
    )
    before = (
        lax.dot_general(layer_in, features, contract_first, preferred_element_type=jnp.float32)
        + layer_bias[:, None]
    )
    hidden = jax.nn.silu(before).astype(jnp.bfloat16)
    forcing = lax.dot_general(
        layer_out, hidden, contract_first, preferred_element_type=jnp.float32
    ).reshape(2, levels, cells_east, cells_north)
    east_star = window(padded[0], 0, 0, 1, cells_east, cells_north) + TIME_STEP * advect(
        padded, 0, 1, cells_east, cells_north
    )
    north_star = window(padded[1], 0, 0, 1, cells_east, cells_north) + TIME_STEP * advect(
        padded, 1, 1, cells_east, cells_north
    )
    up_star = model_state[2] + TIME_STEP * (
        advect(padded, 2, 0, cells_east, cells_north) + BUOYANCY * model_state[3] + forcing[1]
    )
    potential_new = model_state[3] + TIME_STEP * (
        advect(padded, 3, 0, cells_east, cells_north) + forcing[0]
    )
    profile = density[:, None, None]
    divergence = (
        0.5 * (east_star[:, 2:, 1:-1] - east_star[:, :-2, 1:-1])
        + 0.5 * (north_star[:, 1:-1, 2:] - north_star[:, 1:-1, :-2])
        + vertical(profile * up_star) / profile
    )
    modal = jnp.einsum("ml,lxy->mxy", mode_forward, divergence, precision=HIGH)
    total_east = cells_east * lax.axis_size("gx")
    total_north = cells_north * lax.axis_size("gy")
    cosine_east, sine_east = tables(total_east)
    cosine_north, sine_north = tables(total_north)
    band_levels = levels // lax.axis_size("gy")
    banded = lax.all_to_all(modal, "gy", split_axis=0, concat_axis=2, tiled=True)
    spec_real = jnp.einsum("kn,lxn->xlk", cosine_north, banded, precision=HIGH).reshape(
        cells_east, band_levels * total_north
    )
    spec_imag = -jnp.einsum("kn,lxn->xlk", sine_north, banded, precision=HIGH).reshape(
        cells_east, band_levels * total_north
    )
    rows_real, rows_imag = (
        lax.all_to_all(spec_real, "gx", split_axis=1, concat_axis=0, tiled=True),
        lax.all_to_all(spec_imag, "gx", split_axis=1, concat_axis=0, tiled=True),
    )
    width_cols = rows_real.shape[1]
    trans_real, trans_imag = complex_pass(
        cosine_east, sine_east, rows_real, rows_imag, "kn,nj->kj", 1
    )
    columns = lax.axis_index("gx") * width_cols + jnp.arange(width_cols, dtype=jnp.int32)
    level_of = lax.axis_index("gy") * band_levels + columns // total_north
    wave_north = columns % total_north
    symbol_east = jnp.sin(jnp.arange(total_east, dtype=jnp.float32) * (2.0 * math.pi / total_east))
    symbol_north = jnp.sin(wave_north.astype(jnp.float32) * (2.0 * math.pi / total_north))
    denominator = (
        rates_for(level_of, mode_rate)[None, :]
        + (symbol_east * symbol_east)[:, None]
        + (symbol_north * symbol_north)[None, :]
    )
    back_real, back_imag = complex_pass(
        cosine_east,
        sine_east,
        -trans_real / denominator,
        -trans_imag / denominator,
        "kn,nj->kj",
        -1,
    )
    back_real = back_real / total_east
    back_imag = back_imag / total_east
    band_shape = (cells_east, band_levels, total_north)
    slope_real = centered(back_real, 0)
    slope_imag = centered(back_imag, 0)
    part_real, part_imag, part_slope_real, part_slope_imag = (
        lax.all_to_all(back_real, "gx", split_axis=0, concat_axis=1, tiled=True),
        lax.all_to_all(back_imag, "gx", split_axis=0, concat_axis=1, tiled=True),
        lax.all_to_all(slope_real, "gx", split_axis=0, concat_axis=1, tiled=True),
        lax.all_to_all(slope_imag, "gx", split_axis=0, concat_axis=1, tiled=True),
    )
    press_band = (
        jnp.einsum("kn,xlk->xln", cosine_north, part_real.reshape(band_shape), precision=HIGH)
        - jnp.einsum("kn,xlk->xln", sine_north, part_imag.reshape(band_shape), precision=HIGH)
    ) / total_north
    slope_east_band = (
        jnp.einsum("kn,xlk->xln", cosine_north, part_slope_real.reshape(band_shape), precision=HIGH)
        - jnp.einsum("kn,xlk->xln", sine_north, part_slope_imag.reshape(band_shape), precision=HIGH)
    ) / total_north
    slope_north_band = centered(press_band, 2)
    pressure_modal, slope_east_modal, slope_north_modal = (
        lax.all_to_all(press_band, "gy", split_axis=2, concat_axis=1, tiled=True),
        lax.all_to_all(slope_east_band, "gy", split_axis=2, concat_axis=1, tiled=True),
        lax.all_to_all(slope_north_band, "gy", split_axis=2, concat_axis=1, tiled=True),
    )
    formula = "ml,xly->mxy"
    pressure = jnp.einsum(formula, mode_back, pressure_modal, precision=HIGH)
    slope_east = jnp.einsum(formula, mode_back, slope_east_modal, precision=HIGH)
    slope_north = jnp.einsum(formula, mode_back, slope_north_modal, precision=HIGH)
    return jnp.stack(
        [
            east_star[:, 1:-1, 1:-1] - slope_east,
            north_star[:, 1:-1, 1:-1] - slope_north,
            up_star - vertical(pressure),
            potential_new,
        ]
    )


def solution(mesh):
    return jax.shard_map(
        on_device,
        mesh=mesh,
        in_specs=(P(None, None, "gx", "gy"), P(), P(), P(), P(), P(), P(), P()),
        out_specs=P(None, None, "gx", "gy"),
        check_vma=False,
    )
```

profile of v0, /device:TPU:0, one launch (start us, length us, event | category | flops | bytes accessed | tf_op | source)
XLA Modules:
  0.0 144.7 jit_solution(3863586760535884843)
XLA Ops:
  0.0 1.2 copy.69
  1.8 5.0 %collective-permute-start.1 = (f32[4,64,2,128]{3,1,2,0:T(8,128)S(1)}, f32[4,64,2,128]{3,1,2,0:T(8,128)S(1)}, u32[]{:S(2)}, u32[]{:S(2)}) collective-permute-start(f32[4,64,2,128]{3,1,2,0:T(8,128)S(1)} %get-tuple-element.23), channel_id=1, source_target_pairs={{2,0},{4,2},{6,4},{8,6},{10,8},{12,10},{14,12},{16,14},{18,16},{20... | collective-permute-start | bytes 786440 | tf_op jit(solution)/shard_map/ppermute | solution.py:22
  6.9 1.2 convolution_bitcast_fusion
  8.1 2.8 %collective-permute-done = f32[4,64,2,128]{3,1,2,0:T(8,128)S(1)} collective-permute-done((f32[4,64,2,128]{3,1,2,0:T(8,128)S(1)}, f32[4,64,2,128]{3,1,2,0:T(8,128)S(1)}, u32[]{:S(2)}, u32[]{:S(2)}) %collective-permute-start) | collective-permute-done | bytes 262176 | tf_op jit(solution)/shard_map/ppermute | solution.py:20
  11.4 1.0 copy.72
  12.4 2.0 %collective-permute-start.2 = (f32[4,64,8,2]{1,2,3,0:T(8,128)}, f32[4,64,8,2]{1,2,3,0:T(8,128)S(1)}, u32[]{:S(2)}, u32[]{:S(2)}) collective-permute-start(f32[4,64,8,2]{1,2,3,0:T(8,128)} %copy.72), channel_id=1, source_target_pairs={{0,1},{1,0},{2,3},{3,2},{4,5},{5,4},{6,7},{7,6},{8,9},{9,8},{10,11... | collective-permute-start | bytes 49160 | tf_op jit(solution)/shard_map/ppermute | solution.py:20
  14.8 1.0 slice_bitcast_fusion.5
  15.8 0.7 collective-permute-done.2
  16.9 2.0 %collective-permute-done.3 = f32[4,64,8,2]{1,2,3,0:T(8,128)} collective-permute-done((f32[4,64,8,2]{1,2,3,0:T(8,128)S(1)}, f32[4,64,8,2]{1,2,3,0:T(8,128)}, u32[]{:S(2)}, u32[]{:S(2)}) %collective-permute-start.3) | collective-permute-done | bytes 16416 | tf_op jit(solution)/shard_map/ppermute | solution.py:22
  18.9 1.1 copy.75
  20.0 0.9 pad_maximum_fusion
  21.6 0.9 fusion.182
  22.5 1.0 broadcast_multiply_fusion
  23.5 1.0 fusion.28
  24.6 0.7 copy-done.4
  25.7 0.7 copy.79
  26.5 3.4 %all-to-all-start = ((f32[64,4,128]{2,1,0:T(4,128)}), f32[64,4,128]{2,1,0:T(4,128)S(1)}, u32[]{:S(2)}, u32[]{:S(2)}) async-start(f32[64,4,128]{2,1,0:T(4,128)} %copy.79), calls=%async_computation | async-start | bytes 262144 | tf_op jit(solution)/shard_map/all_to_all | solution.py:141
  29.9 4.5 %all-to-all-done = f32[64,4,128]{2,1,0:T(4,128)S(1)} async-done(((f32[64,4,128]{2,1,0:T(4,128)}), f32[64,4,128]{2,1,0:T(4,128)S(1)}, u32[]{:S(2)}, u32[]{:S(2)}) %all-to-all-start) | async-done | bytes 131104 | tf_op jit(solution)/shard_map/all_to_all | solution.py:141
  34.5 1.3 convolution_bitcast_fusion.1
  35.9 0.7 copy.81
  36.7 5.0 %all-to-all-start.1 = ((f32[4,16,512]{2,0,1:T(4,128)}), f32[4,16,512]{2,0,1:T(4,128)S(1)}, u32[]{:S(2)}, u32[]{:S(2)}) async-start(f32[4,16,512]{2,0,1:T(4,128)} %copy.81), calls=%async_computation.1 | async-start | bytes 262144 | tf_op jit(solution)/shard_map/all_to_all | solution.py:149
  41.8 1.4 fusion.2
  43.2 0.7 copy.82
  43.9 5.7 %all-to-all-done.1 = f32[4,16,512]{2,0,1:T(4,128)S(1)} async-done(((f32[4,16,512]{2,0,1:T(4,128)}), f32[4,16,512]{2,0,1:T(4,128)S(1)}, u32[]{:S(2)}, u32[]{:S(2)}) %all-to-all-start.1) | async-done | bytes 131104 | tf_op jit(solution)/shard_map/all_to_all | solution.py:149
  49.6 3.5 %all-to-all-start.2 = ((f32[4,16,512]{2,0,1:T(4,128)}), f32[4,16,512]{2,0,1:T(4,128)S(1)}, u32[]{:S(2)}, u32[]{:S(2)}) async-start(f32[4,16,512]{2,0,1:T(4,128)} %copy.82), calls=%async_computation.2 | async-start | bytes 262144 | tf_op jit(solution)/shard_map/all_to_all | solution.py:150
  53.4 7.7 %all-to-all-done.2 = f32[4,16,512]{2,0,1:T(4,128)S(1)} async-done(((f32[4,16,512]{2,0,1:T(4,128)}), f32[4,16,512]{2,0,1:T(4,128)S(1)}, u32[]{:S(2)}, u32[]{:S(2)}) %all-to-all-start.2) | async-done | bytes 131104 | tf_op jit(solution)/shard_map/all_to_all | solution.py:150
  63.2 0.7 fusion.186
  64.3 0.7 all_to_all.141
  65.0 3.5 %all-to-all-start.6 = ((f32[16,4,512]{2,1,0:T(4,128)}), f32[16,4,512]{2,1,0:T(4,128)S(1)}, u32[]{:S(2)}, u32[]{:S(2)}) async-start(f32[16,4,512]{2,1,0:T(4,128)} %all_to_all.141), calls=%async_computation.6 | async-start | bytes 262144 | tf_op jit(solution)/shard_map/all_to_all | solution.py:180
  68.5 0.9 fusion.78
  69.5 0.7 all_to_all.144
  70.2 0.7 mul.335
  70.9 5.6 %all-to-all-done.6 = f32[16,4,512]{2,1,0:T(4,128)S(1)} async-done(((f32[16,4,512]{2,1,0:T(4,128)}), f32[16,4,512]{2,1,0:T(4,128)S(1)}, u32[]{:S(2)}, u32[]{:S(2)}) %all-to-all-start.6) | async-done | bytes 131104 | tf_op jit(solution)/shard_map/all_to_all | solution.py:180
  76.4 3.7 %all-to-all-start.7 = ((f32[16,4,512]{2,1,0:T(4,128)}), f32[16,4,512]{2,1,0:T(4,128)S(1)}, u32[]{:S(2)}, u32[]{:S(2)}) async-start(f32[16,4,512]{2,1,0:T(4,128)} %all_to_all.144), calls=%async_computation.7 | async-start | bytes 262144 | tf_op jit(solution)/shard_map/all_to_all | solution.py:181
  80.2 0.7 mul.333
  81.0 7.1 %all-to-all-done.7 = f32[16,4,512]{2,1,0:T(4,128)S(1)} async-done(((f32[16,4,512]{2,1,0:T(4,128)}), f32[16,4,512]{2,1,0:T(4,128)S(1)}, u32[]{:S(2)}, u32[]{:S(2)}) %all-to-all-start.7) | async-done | bytes 131104 | tf_op jit(solution)/shard_map/all_to_all | solution.py:181
  88.0 3.5 %all-to-all-start.4 = ((f32[16,4,512]{2,1,0:T(4,128)}), f32[16,4,512]{2,1,0:T(4,128)S(1)}, u32[]{:S(2)}, u32[]{:S(2)}) async-start(f32[16,4,512]{2,1,0:T(4,128)} %mul.335), calls=%async_computation.4 | async-start | bytes 262144 | tf_op jit(solution)/shard_map/all_to_all | solution.py:183
  91.6 1.2 fusion.41
  92.9 1.3 fusion
  94.2 5.3 %all-to-all-done.4 = f32[16,4,512]{2,1,0:T(4,128)S(1)} async-done(((f32[16,4,512]{2,1,0:T(4,128)}), f32[16,4,512]{2,1,0:T(4,128)S(1)}, u32[]{:S(2)}, u32[]{:S(2)}) %all-to-all-start.4) | async-done | bytes 131104 | tf_op jit(solution)/shard_map/all_to_all | solution.py:183
  99.5 3.5 %all-to-all-start.3 = ((f32[16,4,512]{2,1,0:T(4,128)}), f32[16,4,512]{2,1,0:T(4,128)S(1)}, u32[]{:S(2)}, u32[]{:S(2)}) async-start(f32[16,4,512]{2,1,0:T(4,128)} %mul.333), calls=%async_computation.3 | async-start | bytes 262144 | tf_op jit(solution)/shard_map/all_to_all | solution.py:182
  103.0 0.7 fusion.189
  103.8 0.8 fusion.190
  104.5 6.3 %all-to-all-done.3 = f32[16,4,512]{2,1,0:T(4,128)S(1)} async-done(((f32[16,4,512]{2,1,0:T(4,128)}), f32[16,4,512]{2,1,0:T(4,128)S(1)}, u32[]{:S(2)}, u32[]{:S(2)}) %all-to-all-start.3) | async-done | bytes 131104 | tf_op jit(solution)/shard_map/all_to_all | solution.py:182
  111.0 1.2 fusion.43
  112.2 1.9 %fusion.1 = f32[4,32,256]{2,1,0:T(8,128)} fusion(f32[4,32,256]{2,1,0:T(8,128)S(1)} %fusion.43, f32[4,32,256]{2,1,0:T(8,128)S(1)} %reshape.104), kind=kOutput, calls=%fused_computation.6 | convolution fusion | flops 101646336 | bytes 393216 | tf_op jit(solution)/shard_map/kn,xlk->xln/dot_general | solution.py:191
  114.1 1.1 copy.85
  115.3 1.0 reshape.115
  116.2 4.0 %all-to-all-start.5 = ((f32[2,1,16384]{2,1,0:T(1,128)}), f32[2,1,16384]{2,1,0:T(1,128)}, u32[]{:S(2)}, u32[]{:S(2)}) async-start(f32[2,1,16384]{2,1,0:T(1,128)} %reshape.115), calls=%async_computation.5 | async-start | bytes 262144 | tf_op jit(solution)/shard_map/all_to_all | solution.py:196
  120.3 1.8 %fusion.79 = f32[4,32,256]{2,1,0:T(8,128)} fusion(f32[4,32,1]{2,1,0:T(8,128)} %get-tuple-element.36, f32[4,32,255]{2,1,0:T(8,128)} %get-tuple-element.38, f32[4,32,255]{2,1,0:T(8,128)} %get-tuple-element.37, f32[4,32,1]{2,1,0:T(8,128)} %get-tuple-element.35), kind=kLoop, calls=%fused_computation.119 | loop fusion | flops 131072 | bytes 393216 | tf_op jit(solution)/shard_map/mul | solution.py:30
  122.0 1.1 copy.89
  123.2 1.0 reshape.113
  124.2 0.7 all-to-all-done.5
  124.8 3.4 %all-to-all-start.8 = ((f32[2,1,16384]{2,1,0:T(1,128)}), f32[2,1,16384]{2,1,0:T(1,128)S(1)}, u32[]{:S(2)}, u32[]{:S(2)}) async-start(f32[2,1,16384]{2,1,0:T(1,128)} %reshape.113), calls=%async_computation.8 | async-start | bytes 262144 | tf_op jit(solution)/shard_map/all_to_all | solution.py:197
  128.2 1.3 fusion.53
  129.7 1.0 reshape.111
  130.7 0.6 broadcast.234
  131.3 2.0 %reduce.2 = f32[2,16384]{1,0:T(2,128)S(1)} reduce(f32[2,1,16384]{2,1,0:T(1,128)} %all-to-all-done.5, f32[]{:T(128)} %broadcast.234), dimensions={1}, to_apply=%all_to_all.137.reduce_sub_computation | reduce | bytes 262148 | tf_op jit(solution)/shard_map/all_to_all | solution.py:196
  133.8 3.4 %all-to-all-start.9 = ((f32[2,1,16384]{2,1,0:T(1,128)}), f32[2,1,16384]{2,1,0:T(1,128)S(1)}, u32[]{:S(2)}, u32[]{:S(2)}) async-start(f32[2,1,16384]{2,1,0:T(1,128)} %reshape.111), calls=%async_computation.9 | async-start | bytes 262144 | tf_op jit(solution)/shard_map/all_to_all | solution.py:195
  137.2 1.1 reduce.1
  138.8 1.2 fusion.6
  140.0 1.2 fusion.4
  141.7 1.0 reduce
  143.6 1.1 copy.94
  (81 shorter events, 9.1 us)
Async XLA Ops:
  0.0 6.9 %copy-start = (bf16[256,256]{1,0:T(8,128)(2,1)S(1)}, bf16[256,256]{1,0:T(8,128)(2,1)}, u32[]{:S(2)}) copy-start(bf16[256,256]{1,0:T(8,128)(2,1)} %param.10) | copy-start | bytes 393220
  0.0 6.8 %copy-start.1 = (f32[4,64,4,128]{3,2,1,0:T(4,128)S(1)}, f32[4,64,4,128]{3,2,1,0:T(4,128)}, u32[]{:S(2)}) copy-start(f32[4,64,4,128]{3,2,1,0:T(4,128)} %param.8) | copy-start | bytes 1572868
  0.0 6.9 %copy-start.12 = (f32[256]{0:T(256)S(1)}, f32[256]{0:T(256)}, u32[]{:S(2)}) copy-start(f32[256]{0:T(256)} %param.11) | copy-start | bytes 3076
  0.0 6.9 %copy-start.10 = (bf16[256,128]{1,0:T(8,128)(2,1)S(1)}, bf16[256,128]{1,0:T(8,128)(2,1)}, u32[]{:S(2)}) copy-start(bf16[256,128]{1,0:T(8,128)(2,1)} %param.12) | copy-start | bytes 196612
  1.2 6.9 %copy-start.2 = (f32[4,64,4,128]{3,1,2,0:T(8,128)}, f32[4,64,4,128]{3,1,2,0:T(8,128)S(1)}, u32[]{:S(2)}) copy-start(f32[4,64,4,128]{3,1,2,0:T(8,128)S(1)} %copy.69) | copy-start | bytes 1572868
  1.2 9.6 %collective-permute-start = (f32[4,64,2,128]{3,1,2,0:T(8,128)S(1)}, f32[4,64,2,128]{3,1,2,0:T(8,128)S(1)}, u32[]{:S(2)}, u32[]{:S(2)}) collective-permute-start(f32[4,64,2,128]{3,1,2,0:T(8,128)S(1)} %get-tuple-element.24), channel_id=1, source_target_pairs={{0,2},{2,4},{4,6},{6,8},{8,10},{10,12},{12,14},{14,16},{16,18},{18... | collective-permute-start | bytes 786440 | tf_op jit(solution)/shard_map/ppermute | solution.py:20
  1.8 9.2 %collective-permute-start.1 = (f32[4,64,2,128]{3,1,2,0:T(8,128)S(1)}, f32[4,64,2,128]{3,1,2,0:T(8,128)S(1)}, u32[]{:S(2)}, u32[]{:S(2)}) collective-permute-start(f32[4,64,2,128]{3,1,2,0:T(8,128)S(1)} %get-tuple-element.23), channel_id=1, source_target_pairs={{2,0},{4,2},{6,4},{8,6},{10,8},{12,10},{14,12},{16,14},{18,16},{20... | collective-permute-start | bytes 786440 | tf_op jit(solution)/shard_map/ppermute | solution.py:22
  12.4 4.1 %collective-permute-start.2 = (f32[4,64,8,2]{1,2,3,0:T(8,128)}, f32[4,64,8,2]{1,2,3,0:T(8,128)S(1)}, u32[]{:S(2)}, u32[]{:S(2)}) collective-permute-start(f32[4,64,8,2]{1,2,3,0:T(8,128)} %copy.72), channel_id=1, source_target_pairs={{0,1},{1,0},{2,3},{3,2},{4,5},{5,4},{6,7},{7,6},{8,9},{9,8},{10,11... | collective-permute-start | bytes 49160 | tf_op jit(solution)/shard_map/ppermute | solution.py:20
  14.7 4.1 %collective-permute-start.3 = (f32[4,64,8,2]{1,2,3,0:T(8,128)S(1)}, f32[4,64,8,2]{1,2,3,0:T(8,128)}, u32[]{:S(2)}, u32[]{:S(2)}) collective-permute-start(f32[4,64,8,2]{1,2,3,0:T(8,128)S(1)} %copy.73), channel_id=1, source_target_pairs={{1,0},{0,1},{3,2},{2,3},{5,4},{4,5},{7,6},{6,7},{9,8},{8,9},{11,10... | collective-permute-start | bytes 49160 | tf_op jit(solution)/shard_map/ppermute | solution.py:22
  21.1 1.4 copy-start.3
  21.2 1.4 copy-start.9
  23.5 1.8 %copy-start.11 = (f32[64,64]{1,0:T(8,128)S(1)}, f32[64,64]{1,0:T(8,128)}, u32[]{:S(2)}) copy-start(f32[64,64]{1,0:T(8,128)} %param.13) | copy-start | bytes 49156
  24.5 0.7 copy-start.4
  24.5 1.2 copy-start.5
  26.5 7.8 %all-to-all-start = ((f32[64,4,128]{2,1,0:T(4,128)}), f32[64,4,128]{2,1,0:T(4,128)S(1)}, u32[]{:S(2)}, u32[]{:S(2)}) async-start(f32[64,4,128]{2,1,0:T(4,128)} %copy.79), calls=%async_computation | async-start | bytes 262144 | tf_op jit(solution)/shard_map/all_to_all | solution.py:141
  34.3 18.9 %copy-start.8 = (f32[64]{0:T(128)S(1)}, f32[64]{0:T(128)}, u32[]{:S(2)}) copy-start(f32[64]{0:T(128)} %param.15) | copy-start | bytes 772
  36.7 13.0 %all-to-all-start.1 = ((f32[4,16,512]{2,0,1:T(4,128)}), f32[4,16,512]{2,0,1:T(4,128)S(1)}, u32[]{:S(2)}, u32[]{:S(2)}) async-start(f32[4,16,512]{2,0,1:T(4,128)} %copy.81), calls=%async_computation.1 | async-start | bytes 262144 | tf_op jit(solution)/shard_map/all_to_all | solution.py:149
  49.6 11.4 %all-to-all-start.2 = ((f32[4,16,512]{2,0,1:T(4,128)}), f32[4,16,512]{2,0,1:T(4,128)S(1)}, u32[]{:S(2)}, u32[]{:S(2)}) async-start(f32[4,16,512]{2,0,1:T(4,128)} %copy.82), calls=%async_computation.2 | async-start | bytes 262144 | tf_op jit(solution)/shard_map/all_to_all | solution.py:150
  65.0 11.4 %all-to-all-start.6 = ((f32[16,4,512]{2,1,0:T(4,128)}), f32[16,4,512]{2,1,0:T(4,128)S(1)}, u32[]{:S(2)}, u32[]{:S(2)}) async-start(f32[16,4,512]{2,1,0:T(4,128)} %all_to_all.141), calls=%async_computation.6 | async-start | bytes 262144 | tf_op jit(solution)/shard_map/all_to_all | solution.py:180
  76.4 11.6 %all-to-all-start.7 = ((f32[16,4,512]{2,1,0:T(4,128)}), f32[16,4,512]{2,1,0:T(4,128)S(1)}, u32[]{:S(2)}, u32[]{:S(2)}) async-start(f32[16,4,512]{2,1,0:T(4,128)} %all_to_all.144), calls=%async_computation.7 | async-start | bytes 262144 | tf_op jit(solution)/shard_map/all_to_all | solution.py:181
  88.0 11.4 %all-to-all-start.4 = ((f32[16,4,512]{2,1,0:T(4,128)}), f32[16,4,512]{2,1,0:T(4,128)S(1)}, u32[]{:S(2)}, u32[]{:S(2)}) async-start(f32[16,4,512]{2,1,0:T(4,128)} %mul.335), calls=%async_computation.4 | async-start | bytes 262144 | tf_op jit(solution)/shard_map/all_to_all | solution.py:183
  99.5 11.4 %all-to-all-start.3 = ((f32[16,4,512]{2,1,0:T(4,128)}), f32[16,4,512]{2,1,0:T(4,128)S(1)}, u32[]{:S(2)}, u32[]{:S(2)}) async-start(f32[16,4,512]{2,1,0:T(4,128)} %mul.333), calls=%async_computation.3 | async-start | bytes 262144 | tf_op jit(solution)/shard_map/all_to_all | solution.py:182
  116.2 8.6 %all-to-all-start.5 = ((f32[2,1,16384]{2,1,0:T(1,128)}), f32[2,1,16384]{2,1,0:T(1,128)}, u32[]{:S(2)}, u32[]{:S(2)}) async-start(f32[2,1,16384]{2,1,0:T(1,128)} %reshape.115), calls=%async_computation.5 | async-start | bytes 262144 | tf_op jit(solution)/shard_map/all_to_all | solution.py:196
  124.8 9.0 %all-to-all-start.8 = ((f32[2,1,16384]{2,1,0:T(1,128)}), f32[2,1,16384]{2,1,0:T(1,128)S(1)}, u32[]{:S(2)}, u32[]{:S(2)}) async-start(f32[2,1,16384]{2,1,0:T(1,128)} %reshape.113), calls=%async_computation.8 | async-start | bytes 262144 | tf_op jit(solution)/shard_map/all_to_all | solution.py:197
  129.7 9.0 %copy-start.7 = (f32[64,64]{1,0:T(8,128)S(1)}, f32[64,64]{1,0:T(8,128)}, u32[]{:S(2)}) copy-start(f32[64,64]{1,0:T(8,128)} %param.14) | copy-start | bytes 49156
  133.8 7.9 %all-to-all-start.9 = ((f32[2,1,16384]{2,1,0:T(1,128)}), f32[2,1,16384]{2,1,0:T(1,128)S(1)}, u32[]{:S(2)}, u32[]{:S(2)}) async-start(f32[2,1,16384]{2,1,0:T(1,128)} %reshape.111), calls=%async_computation.9 | async-start | bytes 262144 | tf_op jit(solution)/shard_map/all_to_all | solution.py:195
  138.6 5.0 %copy-start.6 = (f32[64,4,128]{2,0,1:T(8,128)S(1)}, f32[64,4,128]{2,0,1:T(8,128)}, u32[]{:S(2)}) copy-start(f32[64,4,128]{2,0,1:T(8,128)} %get-tuple-element.6) | copy-start | bytes 393220
where the time goes:
time: 146 us; the launch traced here: 145 us
  waiting for transfers between devices  48.7 us (33%)
  starting transfers between devices  44.5 us (30%)
  local copies, waits for them, and re-layouts  24.4 us (17%)
  matrix products  15.2 us (10%)
  other arithmetic  11.3 us (8%)
    all_to_all x1, waiting for transfers between devices, on_device(): lax.all_to_all(spec_imag, 'gx', split_axis=1, concat_axis=0, tiled=True)  7.67 us
    all_to_all x1, waiting for transfers between devices, on_device(): lax.all_to_all(back_imag, 'gx', split_axis=0, concat_axis=1, tiled=True)  7.08 us
    unnamed x36, local copies, waits for them, and re-layouts  6.92 us
    all_to_all x1, waiting for transfers between devices, on_device(): lax.all_to_all(slope_real, 'gx', split_axis=0, concat_axis=1, tiled=True)  6.34 us
    all_to_all x1, waiting for transfers between devices, on_device(): lax.all_to_all(spec_real, 'gx', split_axis=1, concat_axis=0, tiled=True)  5.73 us
    all_to_all x1, waiting for transfers between devices, on_device(): lax.all_to_all(back_real, 'gx', split_axis=0, concat_axis=1, tiled=True)  5.56 us
    all_to_all x1, waiting for transfers between devices, on_device(): lax.all_to_all(slope_imag, 'gx', split_axis=0, concat_axis=1, tiled=True)  5.3 us
    ppermute x2, starting transfers between devices, extended(): lax.ppermute(head, axis, [((i + 1) % count, i) for i in range(count)])  5.11 us
  transfers between devices with their start and end apart: 14, of which 12 were waited for; matrix products, arithmetic and copies ran while one was open for 18% of the time, Pallas kernels for 0%

commit v1 on v0

--- a/solution.py
+++ b/solution.py
@@ -1,8 +1,12 @@
+import functools
 import math
 
 import jax
 import jax.numpy as jnp
+import numpy as np
 from jax import lax
+from jax.experimental import pallas as pl
+from jax.experimental.pallas import tpu as pltpu
 from jax.sharding import PartitionSpec as P
 
 HIGH = lax.Precision.HIGHEST
@@ -210,9 +214,411 @@
     )
 
 
+F32 = jnp.float32
+BF16 = jnp.bfloat16
+MESH = pl.DeviceIdType.MESH
+
+
+def halves(values):
+    high = values.astype(BF16)
+    return high, (values - high.astype(F32)).astype(BF16)
+
+
+def product(left, right):
+    def dot(a, b):
+        return jnp.dot(a, b, preferred_element_type=F32)
+
+    return dot(left[0], right[0]) + (dot(left[0], right[1]) + dot(left[1], right[0]))
+
+
+def real_basis(length):
+    place = np.arange(length)[:, None]
+    wave = np.arange(length)[None, :]
+    half = length // 2
+    number = np.where(wave <= half, wave, wave - half)
+    angle = (place * number % length) * (2.0 * math.pi / length)
+    basis = np.where(wave <= half, np.cos(angle), np.sin(angle)) * math.sqrt(2.0 / length)
+    basis = np.where((wave == 0) | (wave == half), basis / math.sqrt(2.0), basis)
+    return basis, np.sin(number[0] * (2.0 * math.pi / length)) ** 2
+
+
+def pair(table):
+    high = table.astype(np.float32).astype(jnp.bfloat16)
+    low = (table - high.astype(np.float64)).astype(np.float32).astype(jnp.bfloat16)
+    return np.stack([high, low])
+
+
+def constant_tables(total_east, total_north, cells_east):
+    basis_east, symbol_east = real_basis(total_east)
+    basis_north, symbol_north = real_basis(total_north)
+    blocks = total_east // cells_east
+    gather = np.zeros((2, total_east, blocks, 2, cells_east))
+    spread = np.zeros((blocks, 2, 8, 2, total_east))
+    for mode in range(2):
+        gather[mode, :, :, mode, :] = basis_east.T.reshape(total_east, blocks, cells_east)
+        for slot in range(cells_east + 2):
+            columns = (np.arange(blocks) * cells_east + slot - 1) % total_east
+            spread[:, mode, slot, mode, :] = basis_east[columns]
+    symbol = symbol_east[:, None] + symbol_north[None, :]
+    return (
+        pair(basis_north),
+        pair(basis_north.T),
+        pair(gather.reshape(2 * total_east, -1)),
+        pair(spread.reshape(-1, 2 * total_east)),
+        np.concatenate([symbol, symbol]).astype(np.float32),
+    )
+
+
+def step_kernel(
+    count_east,
+    state_ref,
+    density_ref,
+    layer_in_ref,
+    bias_ref,
+    layer_out_ref,
+    forward_ref,
+    back_ref,
+    rate_ref,
+    north_ref,
+    north_back_ref,
+    gather_ref,
+    spread_ref,
+    symbol_ref,
+    out_ref,
+    own_u,
+    own_vw,
+    own_th,
+    left_u,
+    left_vw,
+    left_th,
+    right_u,
+    right_vw,
+    right_th,
+    edge_out,
+    edge_in,
+    modal_out,
+    modal_in,
+    press_out,
+    press_in,
+    keep,
+    halo_send,
+    halo_recv,
+    swap_send,
+    swap_recv,
+):
+    devices = 2 * count_east
+    gi = lax.axis_index("gx")
+    gj = lax.axis_index("gy")
+    me = gi * 2 + gj
+    other = 1 - gj
+    right = lax.rem(gi + 1, count_east)
+    left = lax.rem(gi + count_east - 1, count_east)
+    barrier = pltpu.get_barrier_semaphore()
+
+    def greet(k, carry):
+        to = lax.rem(me + k, devices)
+        pl.semaphore_signal(barrier, inc=1, device_id=(to // 2, to % 2), device_id_type=MESH)
+        return carry
+
+    lax.fori_loop(1, devices, greet, 0)
+
+    lane = lax.broadcasted_iota(jnp.int32, (64, 128), 1)
+    level = lax.broadcasted_iota(jnp.int32, (64, 128), 0)
+    lane_tall = lax.broadcasted_iota(jnp.int32, (256, 128), 1)
+
+    slabs = [state_ref[pl.ds(x, 256, stride=4), :] for x in range(4)]
+    edges = jnp.zeros((256, 128), F32)
+    for x in range(4):
+        own_u[x * 64 : x * 64 + 64, :] = slabs[x][0:64]
+        own_vw[x * 128 : x * 128 + 128, :] = slabs[x][64:192]
+        own_th[x * 64 : x * 64 + 64, :] = slabs[x][192:256]
+        edges = jnp.where(lane_tall // 4 == x, pltpu.roll(slabs[x], 4 * x + 2, 1), edges)
+    edge_out[...] = edges.T[0:16]
+
+    pl.semaphore_wait(barrier, devices - 1)
+
+    def halo(n, source, target, to_east, to_north):
+        return pltpu.make_async_remote_copy(
+            src_ref=source,
+            dst_ref=target,
+            send_sem=halo_send.at[n],
+            recv_sem=halo_recv.at[n],
+            device_id=(to_east, to_north),
+            device_id_type=MESH,
+        )
+
+    copies = [
+        halo(0, edge_out, edge_in.at[8:24], gi, other),
+        halo(1, edge_out.at[8:16], edge_in.at[0:8], right, other),
+        halo(2, edge_out.at[0:8], edge_in.at[24:32], left, other),
+        halo(3, own_u.at[128:256], left_u, right, gj),
+        halo(4, own_u.at[0:128], right_u, left, gj),
+        halo(5, own_vw.at[384:512], left_vw, right, gj),
+        halo(6, own_vw.at[0:128], right_vw, left, gj),
+        halo(7, own_th.at[192:256], left_th, right, gj),
+        halo(8, own_th.at[0:64], right_th, left, gj),
+    ]
+    for copy in copies:
+        copy.start()
+
+    features = jnp.concatenate([slab.astype(BF16) for slab in slabs], axis=1)
+    first = (((0,), (0,)), ((), ()))
+    bias = jnp.broadcast_to(bias_ref[...], (128, 256)).T
+    before = lax.dot_general(layer_in_ref[...], features, first, preferred_element_type=F32)
+    before = before + jnp.concatenate([bias] * 4, axis=1)
+    hidden = (before / (1.0 + jnp.exp(-before))).astype(BF16)
+    forcing = lax.dot_general(layer_out_ref[...], hidden, first, preferred_element_type=F32)
+    density = jnp.broadcast_to(
+        jnp.concatenate([density_ref[...], jnp.ones((1, 64), F32)], axis=1), (128, 128)
+    ).T[0:64]
+    inverse_density = 1.0 / density
+    modes = lax.broadcasted_iota(jnp.int32, (1, 64), 1)
+    rates = rate_ref[...]
+    rate_low = jnp.sum(jnp.where(modes == 2 * me, rates, 0.0), axis=1, keepdims=True)
+    rate_high = jnp.sum(jnp.where(modes == 2 * me + 1, rates, 0.0), axis=1, keepdims=True)
+    tall = lax.broadcasted_iota(jnp.int32, (128, 256), 0)
+    green = -1.0 / (jnp.where(tall < 64, rate_low, rate_high) + symbol_ref[...])
+
+    def dz(values):
+        up = jnp.where(level == 63, 0.0, pltpu.roll(values, 63, 0))
+        down = jnp.where(level == 0, 0.0, pltpu.roll(values, 1, 0))
+        return 0.5 * (up - down)
+
+    def dy(values, south, north):
+        ahead = jnp.where(lane == 127, north, pltpu.roll(values, 127, 1))
+        behind = jnp.where(lane == 0, south, pltpu.roll(values, 1, 1))
+        return 0.5 * (ahead - behind)
+
+    def column(values, c):
+        return jnp.broadcast_to(values[:, c : c + 1], (64, 128))
+
+    for n in range(7):
+        copies[n].wait()
+
+    halo_cols = jnp.concatenate([edge_in[...], jnp.zeros((96, 256), F32)], axis=0).T
+    halo_u, halo_v, halo_w, halo_th = [halo_cols[f * 64 : f * 64 + 64] for f in range(4)]
+    own_edges_v = edges[64:128]
+
+    def shift(values, by):
+        return pltpu.roll(values, by % 128, 1)
+
+    is_south = lane % 4 == 1
+    ahead = jnp.where(is_south, shift(own_edges_v, 7), shift(halo_v, -1))
+    behind = jnp.where(is_south, shift(halo_v, 1), shift(own_edges_v, 9))
+    outside_v = halo_v - TIME_STEP * (
+        halo_u * (0.5 * (shift(halo_v, -4) - shift(halo_v, 4)))
+        + halo_v * (0.5 * (ahead - behind))
+        + halo_w * dz(halo_v)
+    )
+
+    u = {x: slabs[x][0:64] for x in range(4)}
+    v = {x: slabs[x][64:128] for x in range(4)}
+    w = {x: slabs[x][128:192] for x in range(4)}
+    th = {x: slabs[x][192:256] for x in range(4)}
+    u[-2], u[-1] = left_u[0:64], left_u[64:128]
+    u[4], u[5] = right_u[0:64], right_u[64:128]
+    v[-1], w[-1] = left_vw[0:64], left_vw[64:128]
+    v[4], w[4] = right_vw[0:64], right_vw[64:128]
+
+    def tendency(f, cols, x):
+        south, north = column(cols, 9 + 4 * x), column(cols, 10 + 4 * x)
+        return -(
+            u[x] * (0.5 * (f[x + 1] - f[x - 1])) + v[x] * dy(f[x], south, north) + w[x] * dz(f[x])
+        )
+
+    east_star = {x: u[x] + TIME_STEP * tendency(u, halo_u, x) for x in range(-1, 5)}
+    pieces = []
+    for x in range(4):
+        north_star = v[x] + TIME_STEP * tendency(v, halo_v, x)
+        heat = forcing[0:64, x * 128 : x * 128 + 128]
+        lift = forcing[64:128, x * 128 : x * 128 + 128]
+        up_star = w[x] + TIME_STEP * (tendency(w, halo_w, x) + BUOYANCY * th[x] + lift)
+        keep[x, 0] = east_star[x]
+        keep[x, 1] = north_star
+        keep[x, 2] = up_star
+        keep[x, 3] = heat
+        pieces.append(
+            0.5 * (east_star[x + 1] - east_star[x - 1])
+            + dy(north_star, column(outside_v, 9 + 4 * x), column(outside_v, 10 + 4 * x))
+            + dz(density * up_star) * inverse_density
+        )
+    modal = product(halves(forward_ref[...]), halves(jnp.concatenate(pieces, axis=1)))
+    for x in range(4):
+        modal_out[pl.ds(x, 64, stride=4), :] = modal[:, x * 128 : x * 128 + 128]
+
+    def exchange(n, source, target, rows, from_place, to_place):
+        def send(k, carry):
+            to = lax.rem(me + k, devices)
+            pltpu.make_async_remote_copy(
+                src_ref=source.at[pl.ds(pl.multiple_of(from_place(to), rows), rows)],
+                dst_ref=target.at[pl.ds(pl.multiple_of(to_place(me), rows), rows)],
+                send_sem=swap_send.at[n],
+                recv_sem=swap_recv.at[n],
+                device_id=(to // 2, to % 2),
+                device_id_type=MESH,
+            ).start()
+            return carry
+
+        lax.fori_loop(1, devices, send, 0)
+        target[pl.ds(pl.multiple_of(to_place(me), rows), rows), :] = source[
+            pl.ds(pl.multiple_of(from_place(me), rows), rows), :
+        ]
+
+    def arrive(n, source, target, rows):
+        total = (devices - 1) * rows
+        pltpu.make_async_remote_copy(
+            src_ref=source.at[0:total],
+            dst_ref=target.at[0:total],
+            send_sem=swap_send.at[n],
+            recv_sem=swap_recv.at[n],
+            device_id=(right, gj),
+            device_id_type=MESH,
+        ).wait()
+
+    half_rows = 8 * count_east
+    exchange(
+        0,
+        modal_out,
+        modal_in,
+        8,
+        lambda d: d * 8,
+        lambda d: (d % 2) * half_rows + (d // 2) * 8,
+    )
+
+    for n in range(7, 9):
+        copies[n].wait()
+    th[-1], th[4] = left_th[...], right_th[...]
+    for x in range(4):
+        out_ref[pl.ds(768 + x, 64, stride=4), :] = th[x] + TIME_STEP * (
+            tendency(th, halo_th, x) + keep[x, 3]
+        )
+
+    arrive(0, modal_out, modal_in, 8)
+
+    rows = jnp.concatenate([modal_in[0:half_rows], modal_in[half_rows : 2 * half_rows]], axis=1)
+    spectral = product(halves(rows), (north_ref[0], north_ref[1]))
+    spectral = product((gather_ref[0], gather_ref[1]), halves(spectral)) * green
+    spread = product((spread_ref[0], spread_ref[1]), halves(spectral))
+    press = product(halves(spread), (north_back_ref[0], north_back_ref[1]))
+    tall_rows = 16 * count_east
+    groups = tall_rows // 8
+    slot = lax.broadcasted_iota(jnp.int32, (tall_rows, 128), 0) % 8
+    wide_lane = lax.broadcasted_iota(jnp.int32, (tall_rows, 128), 1)
+    inside = (slot >= 1) & (slot <= 4)
+    at_south = inside & (wide_lane == slot - 1)
+    at_north = inside & (wide_lane == slot + 3)
+    for j in range(2):
+        south_at, north_at = (255, 128) if j == 0 else (127, 0)
+        picked = jnp.where(at_south, press[:, south_at : south_at + 1], 0.0) + jnp.where(
+            at_north, press[:, north_at : north_at + 1], 0.0
+        )
+        total = jnp.sum(picked.reshape(groups, 8, 128), axis=1, keepdims=True)
+        total = jnp.broadcast_to(total, (groups, 8, 128)).reshape(tall_rows, 128)
+        press_out[j * tall_rows : (j + 1) * tall_rows, :] = jnp.where(
+            slot == 6, total, press[:, j * 128 : j * 128 + 128]
+        )
+    exchange(
+        1,
+        press_out,
+        press_in,
+        16,
+        lambda d: (d % 2) * tall_rows + (d // 2) * 16,
+        lambda d: d * 16,
+    )
+    back = halves(back_ref[...])
+    arrive(1, press_out, press_in, 16)
+    modal_press = jnp.concatenate(
+        [press_in[pl.ds(s, 64, stride=8), :] for s in range(7)], axis=1
+    )
+    full = product(back, halves(modal_press))
+    at = [full[:, s * 128 : s * 128 + 128] for s in range(7)]
+    for x in range(4):
+        out_ref[pl.ds(x, 64, stride=4), :] = keep[x, 0] - 0.5 * (at[x + 2] - at[x])
+        out_ref[pl.ds(256 + x, 64, stride=4), :] = keep[x, 1] - dy(
+            at[x + 1], column(at[6], x), column(at[6], 4 + x)
+        )
+        out_ref[pl.ds(512 + x, 64, stride=4), :] = keep[x, 2] - dz(at[x + 1])
+
+
+def in_one_kernel(
+    count_east,
+    model_state,
+    density,
+    layer_in,
+    layer_bias,
+    layer_out,
+    mode_forward,
+    mode_back,
+    mode_rate,
+):
+    shape = model_state.shape
+    devices = 2 * count_east
+    tables_held = constant_tables(shape[2] * count_east, shape[3] * 2, shape[2])
+    vmem = pl.BlockSpec(memory_space=pltpu.VMEM)
+
+    def held(*extent):
+        return pltpu.VMEM(extent, F32)
+
+    out = pl.pallas_call(
+        functools.partial(step_kernel, count_east),
+        out_shape=jax.ShapeDtypeStruct((1024, 128), F32),
+        in_specs=[vmem] * 13,
+        out_specs=vmem,
+        scratch_shapes=[
+            held(256, 128),
+            held(512, 128),
+            held(256, 128),
+            held(128, 128),
+            held(128, 128),
+            held(64, 128),
+            held(128, 128),
+            held(128, 128),
+            held(64, 128),
+            held(16, 256),
+            held(32, 256),
+            held(8 * devices, 128),
+            held(8 * devices, 128),
+            held(16 * devices, 128),
+            held(16 * devices, 128),
+            held(4, 4, 64, 128),
+            pltpu.SemaphoreType.DMA((9,)),
+            pltpu.SemaphoreType.DMA((9,)),
+            pltpu.SemaphoreType.DMA((2,)),
+            pltpu.SemaphoreType.DMA((2,)),
+        ],
+        compiler_params=pltpu.CompilerParams(
+            collective_id=0, has_side_effects=True, vmem_limit_bytes=32 * 1024 * 1024
+        ),
+    )(
+        model_state.reshape(1024, 128),
+        density.reshape(1, -1),
+        layer_in,
+        layer_bias.reshape(1, -1),
+        layer_out,
+        mode_forward,
+        mode_back,
+        mode_rate.reshape(1, -1),
+        *tables_held,
+    )
+    return out.reshape(shape)
+
+
 def solution(mesh):
+    count_east, count_north = mesh.shape["gx"], mesh.shape["gy"]
+
+    def step(model_state, density, layer_in, *rest):
+        fits = (
+            model_state.shape == (4, 64, 4, 128)
+            and layer_in.shape[1] == 256
+            and count_north == 2
+            and count_east == 16
+        )
+        if fits:
+            return in_one_kernel(count_east, model_state, density, layer_in, *rest)
+        return on_device(model_state, density, layer_in, *rest)
+
     return jax.shard_map(
-        on_device,
+        step,
         mesh=mesh,
         in_specs=(P(None, None, "gx", "gy"), P(), P(), P(), P(), P(), P(), P()),
         out_specs=P(None, None, "gx", "gy"),

time: 146 us -> 36.9 us (0.25)
  the two profiles are of different devices: /device:TPU:0 before, /device:TPU:11 now
where the time goes in v1:
time: 36.9 us; the launch traced here: 36.4 us
  Pallas kernels  26 us (70%)
  local copies, waits for them, and re-layouts  10.3 us (28%)
    pallas_call x1, Pallas kernels, in_one_kernel(): pl.pallas_call(functools.partial(step_kernel, count_east), out_shape=jax....  26 us
    unnamed x27, local copies, waits for them, and re-layouts  10.3 us

profile of v1, /device:TPU:11, one launch (start us, length us, event | category | flops | bytes accessed | tf_op | source)
XLA Modules:
  0.0 36.4 jit_solution(11224774534271728038)
XLA Ops:
  0.0 0.0 copy-start.12
  0.0 0.0 copy-start.10
  0.0 0.0 copy-start.11
  0.0 0.6 %copy-done.12 = f32[64]{0:T(128)S(1)} copy-done((f32[64]{0:T(128)S(1)}, f32[64]{0:T(128)}, u32[]{:S(2)}) %copy-start.12) | copy-done | bytes 280
  0.7 0.0 copy-done.10
  0.7 0.0 copy-done.11
  0.7 0.0 copy-start
  0.7 1.0 %copy-done = f32[4,64,4,128]{3,2,1,0:T(4,128)S(1)} copy-done((f32[4,64,4,128]{3,2,1,0:T(4,128)S(1)}, f32[4,64,4,128]{3,2,1,0:T(4,128)}, u32[]{:S(2)}) %copy-start) | copy-done | bytes 524312
  1.7 0.0 copy-start.1
  1.7 0.9 %copy-done.1 = bf16[2,256,256]{2,1,0:T(8,128)(2,1)S(1)} copy-done((bf16[2,256,256]{2,1,0:T(8,128)(2,1)S(1)}, bf16[2,256,256]{2,1,0:T(8,128)(2,1)}, u32[]{:S(2)}) %copy-start.1) | copy-done | bytes 262168
  2.7 0.0 copy-start.2
  2.7 0.9 %copy-done.2 = bf16[2,256,256]{2,1,0:T(8,128)(2,1)S(1)} copy-done((bf16[2,256,256]{2,1,0:T(8,128)(2,1)S(1)}, bf16[2,256,256]{2,1,0:T(8,128)(2,1)}, u32[]{:S(2)}) %copy-start.2) | copy-done | bytes 262168
  3.6 0.0 copy-start.3
  3.6 0.9 %copy-done.3 = bf16[256,256]{1,0:T(8,128)(2,1)S(1)} copy-done((bf16[256,256]{1,0:T(8,128)(2,1)S(1)}, bf16[256,256]{1,0:T(8,128)(2,1)}, u32[]{:S(2)}) %copy-start.3) | copy-done | bytes 131096
  4.5 0.0 copy-start.4
  4.5 0.9 %copy-done.4 = f32[128,256]{1,0:T(8,128)S(1)} copy-done((f32[128,256]{1,0:T(8,128)S(1)}, f32[128,256]{1,0:T(8,128)}, u32[]{:S(2)}) %copy-start.4) | copy-done | bytes 131096
  5.5 0.0 copy-start.5
  5.5 0.9 %copy-done.5 = bf16[2,256,128]{2,1,0:T(8,128)(2,1)S(1)} copy-done((bf16[2,256,128]{2,1,0:T(8,128)(2,1)S(1)}, bf16[2,256,128]{2,1,0:T(8,128)(2,1)}, u32[]{:S(2)}) %copy-start.5) | copy-done | bytes 131096
  6.4 0.0 copy-start.6
  6.4 0.8 %copy-done.6 = bf16[256,128]{1,0:T(8,128)(2,1)S(1)} copy-done((bf16[256,128]{1,0:T(8,128)(2,1)S(1)}, bf16[256,128]{1,0:T(8,128)(2,1)}, u32[]{:S(2)}) %copy-start.6) | copy-done | bytes 65560
  7.2 0.0 copy-start.7
  7.2 0.8 %copy-done.7 = bf16[2,128,128]{2,1,0:T(8,128)(2,1)S(1)} copy-done((bf16[2,128,128]{2,1,0:T(8,128)(2,1)S(1)}, bf16[2,128,128]{2,1,0:T(8,128)(2,1)}, u32[]{:S(2)}) %copy-start.7) | copy-done | bytes 65560
  8.0 0.0 copy-start.8
  8.0 0.8 %copy-done.8 = f32[64,64]{1,0:T(8,128)S(1)} copy-done((f32[64,64]{1,0:T(8,128)S(1)}, f32[64,64]{1,0:T(8,128)}, u32[]{:S(2)}) %copy-start.8) | copy-done | bytes 16408
  8.8 0.0 copy-start.9
  8.8 0.8 %copy-done.9 = f32[64,64]{1,0:T(8,128)S(1)} copy-done((f32[64,64]{1,0:T(8,128)S(1)}, f32[64,64]{1,0:T(8,128)}, u32[]{:S(2)}) %copy-start.9) | copy-done | bytes 16408
  9.6 26.0 %shard_map.127 = f32[1024,128]{1,0:T(8,128)S(1)} custom-call(f32[1024,128]{1,0:T(8,128)S(1)} %bitcast.6, f32[1,64]{1,0:T(1,128)S(1)} %bitcast.8, bf16[256,256]{1,0:T(8,128)(2,1)S(1)} %copy-done.3, f32[1,256]{1,0:T(1,128)S(1)} %bitcast.7, bf16[256,128]{1,0:T(8,128)(2,1)S(1)} %copy-done.6, f32[64,64]{1,0:T(8,128)S(1)} %copy-done.8, f32[64,64]{1,0:T(8,128)S(1)} %copy-done.9, ...), custom_call_target="tpu_custom_call" | custom-call | tf_op jit(solution)/shard_map/pallas_call | solution.py:562
  35.6 0.8 %copy.15 = f32[4,64,4,128]{3,2,1,0:T(4,128)} copy(f32[4,64,4,128]{3,2,1,0:T(4,128)S(1)} %bitcast.5) | data formatting | bytes 1048576
Async XLA Ops:
  0.0 0.7 %copy-start.12 = (f32[64]{0:T(128)S(1)}, f32[64]{0:T(128)}, u32[]{:S(2)}) copy-start(f32[64]{0:T(128)} %param.20) | copy-start | bytes 772
  0.0 0.7 %copy-start.10 = (f32[256]{0:T(256)S(1)}, f32[256]{0:T(256)}, u32[]{:S(2)}) copy-start(f32[256]{0:T(256)} %param.16) | copy-start | bytes 3076
  0.0 0.7 %copy-start.11 = (f32[64]{0:T(128)S(1)}, f32[64]{0:T(128)}, u32[]{:S(2)}) copy-start(f32[64]{0:T(128)} %param.14) | copy-start | bytes 772
  0.7 1.0 %copy-start = (f32[4,64,4,128]{3,2,1,0:T(4,128)S(1)}, f32[4,64,4,128]{3,2,1,0:T(4,128)}, u32[]{:S(2)}) copy-start(f32[4,64,4,128]{3,2,1,0:T(4,128)} %param.13) | copy-start | bytes 1572868
  1.7 0.9 %copy-start.1 = (bf16[2,256,256]{2,1,0:T(8,128)(2,1)S(1)}, bf16[2,256,256]{2,1,0:T(8,128)(2,1)}, u32[]{:S(2)}) copy-start(bf16[2,256,256]{2,1,0:T(8,128)(2,1)} %constant.11.clone.north_back_ref) | copy-start | bytes 786436
  2.7 0.9 %copy-start.2 = (bf16[2,256,256]{2,1,0:T(8,128)(2,1)S(1)}, bf16[2,256,256]{2,1,0:T(8,128)(2,1)}, u32[]{:S(2)}) copy-start(bf16[2,256,256]{2,1,0:T(8,128)(2,1)} %constant.10.clone.north_ref) | copy-start | bytes 786436
  3.6 0.9 %copy-start.3 = (bf16[256,256]{1,0:T(8,128)(2,1)S(1)}, bf16[256,256]{1,0:T(8,128)(2,1)}, u32[]{:S(2)}) copy-start(bf16[256,256]{1,0:T(8,128)(2,1)} %layer_in_ref.1) | copy-start | bytes 393220
  4.5 0.9 %copy-start.4 = (f32[128,256]{1,0:T(8,128)S(1)}, f32[128,256]{1,0:T(8,128)}, u32[]{:S(2)}) copy-start(f32[128,256]{1,0:T(8,128)} %constant.14.clone.symbol_ref) | copy-start | bytes 393220
  5.5 0.9 %copy-start.5 = (bf16[2,256,128]{2,1,0:T(8,128)(2,1)S(1)}, bf16[2,256,128]{2,1,0:T(8,128)(2,1)}, u32[]{:S(2)}) copy-start(bf16[2,256,128]{2,1,0:T(8,128)(2,1)} %constant.13.clone.spread_ref) | copy-start | bytes 393220
  6.4 0.8 %copy-start.6 = (bf16[256,128]{1,0:T(8,128)(2,1)S(1)}, bf16[256,128]{1,0:T(8,128)(2,1)}, u32[]{:S(2)}) copy-start(bf16[256,128]{1,0:T(8,128)(2,1)} %layer_out_ref.1) | copy-start | bytes 196612
  7.2 0.8 %copy-start.7 = (bf16[2,128,128]{2,1,0:T(8,128)(2,1)S(1)}, bf16[2,128,128]{2,1,0:T(8,128)(2,1)}, u32[]{:S(2)}) copy-start(bf16[2,128,128]{2,1,0:T(8,128)(2,1)} %constant.12.clone.gather_ref) | copy-start | bytes 196612
  8.0 0.8 %copy-start.8 = (f32[64,64]{1,0:T(8,128)S(1)}, f32[64,64]{1,0:T(8,128)}, u32[]{:S(2)}) copy-start(f32[64,64]{1,0:T(8,128)} %forward_ref.1) | copy-start | bytes 49156
  8.8 0.8 %copy-start.9 = (f32[64,64]{1,0:T(8,128)S(1)}, f32[64,64]{1,0:T(8,128)}, u32[]{:S(2)}) copy-start(f32[64,64]{1,0:T(8,128)} %back_ref.1) | copy-start | bytes 49156

commit v2 on v1

--- a/solution.py
+++ b/solution.py
@@ -242,10 +242,14 @@
     return basis, np.sin(number[0] * (2.0 * math.pi / length)) ** 2
 
 
+def lanes_of(table):
+    return np.concatenate([table[:, c : c + 128] for c in range(0, table.shape[1], 128)])
+
+
 def pair(table):
     high = table.astype(np.float32).astype(jnp.bfloat16)
     low = (table - high.astype(np.float64)).astype(np.float32).astype(jnp.bfloat16)
-    return np.stack([high, low])
+    return np.concatenate([lanes_of(high), lanes_of(low)])
 
 
 def constant_tables(total_east, total_north, cells_east):
@@ -261,30 +265,32 @@
             spread[:, mode, slot, mode, :] = basis_east[columns]
     symbol = symbol_east[:, None] + symbol_north[None, :]
     return (
-        pair(basis_north),
-        pair(basis_north.T),
-        pair(gather.reshape(2 * total_east, -1)),
-        pair(spread.reshape(-1, 2 * total_east)),
-        np.concatenate([symbol, symbol]).astype(np.float32),
+        np.concatenate(
+            [
+                pair(basis_north),
+                pair(gather.reshape(2 * total_east, -1)),
+                pair(spread.reshape(-1, 2 * total_east)),
+                pair(basis_north.T),
+            ]
+        ),
+        lanes_of(np.concatenate([symbol, symbol])).astype(np.float32),
     )
 
 
 def step_kernel(
     count_east,
-    state_ref,
-    density_ref,
-    layer_in_ref,
-    bias_ref,
-    layer_out_ref,
-    forward_ref,
-    back_ref,
-    rate_ref,
-    north_ref,
-    north_back_ref,
-    gather_ref,
-    spread_ref,
-    symbol_ref,
+    *refs,
+):
+    operands, out_ref, held = refs[:10], refs[10], refs[11:21]
+    step_body(count_east, operands, held, out_ref, *refs[21:])
+
+
+def step_body(
+    count_east,
+    operands,
+    held,
     out_ref,
+    fetch_sem,
     own_u,
     own_vw,
     own_th,
@@ -313,19 +319,39 @@
     other = 1 - gj
     right = lax.rem(gi + 1, count_east)
     left = lax.rem(gi + count_east - 1, count_east)
+    (
+        state_ref,
+        layer_in_ref,
+        bias_ref,
+        layer_out_ref,
+        density_ref,
+        rate_ref,
+        symbol_ref,
+        forward_ref,
+        table_ref,
+        back_ref,
+    ) = held
+    fetches = [
+        pltpu.make_async_copy(source, target, fetch_sem.at[n])
+        for n, (source, target) in enumerate(zip(operands, held))
+    ]
+    for fetch in fetches:
+        fetch.start()
     barrier = pltpu.get_barrier_semaphore()
 
-    def greet(k, carry):
-        to = lax.rem(me + k, devices)
-        pl.semaphore_signal(barrier, inc=1, device_id=(to // 2, to % 2), device_id_type=MESH)
-        return carry
-
-    lax.fori_loop(1, devices, greet, 0)
+    def partner(steps, across):
+        return lax.rem(gi + steps, count_east), (gj if across == 0 else other)
+
+    partners = [(k, a) for k in range(count_east) for a in range(2) if k or a]
+    partners.sort(key=lambda entry: abs(2 * entry[0] - count_east))
+    for entry in partners:
+        pl.semaphore_signal(barrier, inc=1, device_id=partner(*entry), device_id_type=MESH)
 
     lane = lax.broadcasted_iota(jnp.int32, (64, 128), 1)
     level = lax.broadcasted_iota(jnp.int32, (64, 128), 0)
     lane_tall = lax.broadcasted_iota(jnp.int32, (256, 128), 1)
 
+    fetches[0].wait()
     slabs = [state_ref[pl.ds(x, 256, stride=4), :] for x in range(4)]
     edges = jnp.zeros((256, 128), F32)
     for x in range(4):
@@ -361,6 +387,8 @@
     for copy in copies:
         copy.start()
 
+    for n in range(1, 7):
+        fetches[n].wait()
     features = jnp.concatenate([slab.astype(BF16) for slab in slabs], axis=1)
     first = (((0,), (0,)), ((), ()))
     bias = jnp.broadcast_to(bias_ref[...], (128, 256)).T
@@ -376,8 +404,9 @@
     rates = rate_ref[...]
     rate_low = jnp.sum(jnp.where(modes == 2 * me, rates, 0.0), axis=1, keepdims=True)
     rate_high = jnp.sum(jnp.where(modes == 2 * me + 1, rates, 0.0), axis=1, keepdims=True)
+    symbol = jnp.concatenate([symbol_ref[0:128], symbol_ref[128:256]], axis=1)
     tall = lax.broadcasted_iota(jnp.int32, (128, 256), 0)
-    green = -1.0 / (jnp.where(tall < 64, rate_low, rate_high) + symbol_ref[...])
+    green = -1.0 / (jnp.where(tall < 64, rate_low, rate_high) + symbol)
 
     def dz(values):
         up = jnp.where(level == 63, 0.0, pltpu.roll(values, 63, 0))
@@ -442,27 +471,29 @@
             + dy(north_star, column(outside_v, 9 + 4 * x), column(outside_v, 10 + 4 * x))
             + dz(density * up_star) * inverse_density
         )
+    fetches[7].wait()
     modal = product(halves(forward_ref[...]), halves(jnp.concatenate(pieces, axis=1)))
     for x in range(4):
         modal_out[pl.ds(x, 64, stride=4), :] = modal[:, x * 128 : x * 128 + 128]
 
     def exchange(n, source, target, rows, from_place, to_place):
-        def send(k, carry):
-            to = lax.rem(me + k, devices)
+        def landing(i, j):
+            return pl.ds(pl.multiple_of(to_place(i, j), rows), rows)
+
+        def leaving(i, j):
+            return pl.ds(pl.multiple_of(from_place(i, j), rows), rows)
+
+        for entry in partners:
+            to = partner(*entry)
             pltpu.make_async_remote_copy(
-                src_ref=source.at[pl.ds(pl.multiple_of(from_place(to), rows), rows)],
-                dst_ref=target.at[pl.ds(pl.multiple_of(to_place(me), rows), rows)],
+                src_ref=source.at[leaving(*to)],
+                dst_ref=target.at[landing(gi, gj)],
                 send_sem=swap_send.at[n],
                 recv_sem=swap_recv.at[n],
-                device_id=(to // 2, to % 2),
+                device_id=to,
                 device_id_type=MESH,
             ).start()
-            return carry
-
-        lax.fori_loop(1, devices, send, 0)
-        target[pl.ds(pl.multiple_of(to_place(me), rows), rows), :] = source[
-            pl.ds(pl.multiple_of(from_place(me), rows), rows), :
-        ]
+        target[landing(gi, gj), :] = source[leaving(gi, gj), :]
 
     def arrive(n, source, target, rows):
         total = (devices - 1) * rows
@@ -481,8 +512,8 @@
         modal_out,
         modal_in,
         8,
-        lambda d: d * 8,
-        lambda d: (d % 2) * half_rows + (d // 2) * 8,
+        lambda i, j: (i * 2 + j) * 8,
+        lambda i, j: j * half_rows + i * 8,
     )
 
     for n in range(7, 9):
@@ -493,13 +524,28 @@
             tendency(th, halo_th, x) + keep[x, 3]
         )
 
+    for n in range(8, 10):
+        fetches[n].wait()
+    wide = 2 * half_rows
+
+    def table(start, height, width):
+        def one(at):
+            pieces = [table_ref[at + c * height : at + (c + 1) * height] for c in range(width)]
+            return pieces[0] if width == 1 else jnp.concatenate(pieces, axis=1)
+
+        return one(start), one(start + height * width)
+
+    north = table(0, wide, 2)
+    gather = table(4 * wide, half_rows, 1)
+    spread_out = table(5 * wide, wide, 1)
+    north_back = table(7 * wide, wide, 2)
     arrive(0, modal_out, modal_in, 8)
 
     rows = jnp.concatenate([modal_in[0:half_rows], modal_in[half_rows : 2 * half_rows]], axis=1)
-    spectral = product(halves(rows), (north_ref[0], north_ref[1]))
-    spectral = product((gather_ref[0], gather_ref[1]), halves(spectral)) * green
-    spread = product((spread_ref[0], spread_ref[1]), halves(spectral))
-    press = product(halves(spread), (north_back_ref[0], north_back_ref[1]))
+    spectral = product(halves(rows), north)
+    spectral = product(gather, halves(spectral)) * green
+    spread = product(spread_out, halves(spectral))
+    press = product(halves(spread), north_back)
     tall_rows = 16 * count_east
     groups = tall_rows // 8
     slot = lax.broadcasted_iota(jnp.int32, (tall_rows, 128), 0) % 8
@@ -522,8 +568,8 @@
         press_out,
         press_in,
         16,
-        lambda d: (d % 2) * tall_rows + (d // 2) * 16,
-        lambda d: d * 16,
+        lambda i, j: j * tall_rows + i * 16,
+        lambda i, j: (i * 2 + j) * 16,
     )
     back = halves(back_ref[...])
     arrive(1, press_out, press_in, 16)
@@ -553,8 +599,19 @@
 ):
     shape = model_state.shape
     devices = 2 * count_east
-    tables_held = constant_tables(shape[2] * count_east, shape[3] * 2, shape[2])
-    vmem = pl.BlockSpec(memory_space=pltpu.VMEM)
+    table, symbol = constant_tables(shape[2] * count_east, shape[3] * 2, shape[2])
+    operands = (
+        model_state.reshape(1024, 128),
+        layer_in,
+        layer_bias.reshape(1, -1),
+        layer_out,
+        density.reshape(1, -1),
+        mode_rate.reshape(1, -1),
+        symbol,
+        mode_forward,
+        table,
+        mode_back,
+    )
 
     def held(*extent):
         return pltpu.VMEM(extent, F32)
@@ -562,9 +619,11 @@
     out = pl.pallas_call(
         functools.partial(step_kernel, count_east),
         out_shape=jax.ShapeDtypeStruct((1024, 128), F32),
-        in_specs=[vmem] * 13,
-        out_specs=vmem,
-        scratch_shapes=[
+        in_specs=[pl.BlockSpec(memory_space=pltpu.HBM)] * len(operands),
+        out_specs=pl.BlockSpec(memory_space=pltpu.VMEM),
+        scratch_shapes=[pltpu.VMEM(operand.shape, operand.dtype) for operand in operands]
+        + [
+            pltpu.SemaphoreType.DMA((len(operands),)),
             held(256, 128),
             held(512, 128),
             held(256, 128),
@@ -587,19 +646,9 @@
             pltpu.SemaphoreType.DMA((2,)),
         ],
         compiler_params=pltpu.CompilerParams(
-            collective_id=0, has_side_effects=True, vmem_limit_bytes=32 * 1024 * 1024
+            collective_id=0, has_side_effects=True, vmem_limit_bytes=63 * 1024 * 1024
         ),
-    )(
-        model_state.reshape(1024, 128),
-        density.reshape(1, -1),
-        layer_in,
-        layer_bias.reshape(1, -1),
-        layer_out,
-        mode_forward,
-        mode_back,
-        mode_rate.reshape(1, -1),
-        *tables_held,
-    )
+    )(*operands)
     return out.reshape(shape)
 
 

time: 36.9 us -> 31.1 us (0.84)
  the two profiles are of different devices: /device:TPU:11 before, /device:TPU:0 now
where the time goes in v2:
time: 31.1 us; the launch traced here: 30.9 us
  Pallas kernels  29 us (93%)
  local copies, waits for them, and re-layouts  1.87 us (6%)
    pallas_call x1, Pallas kernels, in_one_kernel(): pl.pallas_call(functools.partial(step_kernel, count_east), out_shape=jax....  29 us
    unnamed x1, local copies, waits for them, and re-layouts  1.87 us

profile of v2, /device:TPU:0, one launch (start us, length us, event | category | flops | bytes accessed | tf_op | source)
XLA Modules:
  0.0 30.9 jit_solution(11367291163848918387)
XLA Ops:
  0.0 29.0 %shard_map.100 = f32[1024,128]{1,0:T(8,128)} custom-call(f32[1024,128]{1,0:T(8,128)} %bitcast.6, bf16[256,256]{1,0:T(8,128)(2,1)} %refs_1_.1, f32[1,256]{1,0:T(1,128)} %bitcast.7, bf16[256,128]{1,0:T(8,128)(2,1)} %refs_3_.1, f32[1,64]{1,0:T(1,128)} %bitcast.8, f32[1,64]{1,0:T(1,128)} %bitcast.9, f32[256,128]{1,0:T(8,128)} %constant.4.clone.refs_6_, ...), custom_call_target="tpu_custom_call" | custom-call | tf_op jit(solution)/shard_map/pallas_call | solution.py:619
  29.0 1.9 %copy.12 = f32[4,64,4,128]{3,2,1,0:T(4,128)} copy(f32[4,64,4,128]{3,2,1,0:T(4,128)} %bitcast.5) | data formatting | bytes 1048576

commit v3 on v2

--- a/solution.py
+++ b/solution.py
@@ -257,19 +257,15 @@
     basis_north, symbol_north = real_basis(total_north)
     blocks = total_east // cells_east
     gather = np.zeros((2, total_east, blocks, 2, cells_east))
-    spread = np.zeros((blocks, 2, 8, 2, total_east))
     for mode in range(2):
         gather[mode, :, :, mode, :] = basis_east.T.reshape(total_east, blocks, cells_east)
-        for slot in range(cells_east + 2):
-            columns = (np.arange(blocks) * cells_east + slot - 1) % total_east
-            spread[:, mode, slot, mode, :] = basis_east[columns]
     symbol = symbol_east[:, None] + symbol_north[None, :]
     return (
         np.concatenate(
             [
                 pair(basis_north),
                 pair(gather.reshape(2 * total_east, -1)),
-                pair(spread.reshape(-1, 2 * total_east)),
+                pair(gather.reshape(2 * total_east, -1).T),
                 pair(basis_north.T),
             ]
         ),
@@ -281,15 +277,15 @@
     count_east,
     *refs,
 ):
-    operands, out_ref, held = refs[:10], refs[10], refs[11:21]
-    step_body(count_east, operands, held, out_ref, *refs[21:])
+    operands, outs, held = refs[:10], refs[10:13], refs[13:23]
+    step_body(count_east, operands, held, outs, *refs[23:])
 
 
 def step_body(
     count_east,
     operands,
     held,
-    out_ref,
+    outs,
     fetch_sem,
     own_u,
     own_vw,
@@ -307,11 +303,18 @@
     press_out,
     press_in,
     keep,
+    out_ref,
+    planes,
+    strip,
+    store_sem,
     halo_send,
     halo_recv,
     swap_send,
     swap_recv,
+    plane_send,
+    plane_recv,
 ):
+    result, sides, strip_in = outs
     devices = 2 * count_east
     gi = lax.axis_index("gx")
     gj = lax.axis_index("gy")
@@ -537,8 +540,17 @@
 
     north = table(0, wide, 2)
     gather = table(4 * wide, half_rows, 1)
-    spread_out = table(5 * wide, wide, 1)
-    north_back = table(7 * wide, wide, 2)
+    spread_out = table(5 * wide, half_rows, 1)
+    north_back = table(6 * wide, wide, 2)
+    stores = [
+        pltpu.make_async_copy(
+            out_ref.at[f * 256 : f * 256 + 256],
+            result.at[f * 256 : f * 256 + 256],
+            store_sem.at[f],
+        )
+        for f in range(4)
+    ]
+    stores[3].start()
     arrive(0, modal_out, modal_in, 8)
 
     rows = jnp.concatenate([modal_in[0:half_rows], modal_in[half_rows : 2 * half_rows]], axis=1)
@@ -546,44 +558,108 @@
     spectral = product(gather, halves(spectral)) * green
     spread = product(spread_out, halves(spectral))
     press = product(halves(spread), north_back)
-    tall_rows = 16 * count_east
-    groups = tall_rows // 8
-    slot = lax.broadcasted_iota(jnp.int32, (tall_rows, 128), 0) % 8
-    wide_lane = lax.broadcasted_iota(jnp.int32, (tall_rows, 128), 1)
-    inside = (slot >= 1) & (slot <= 4)
-    at_south = inside & (wide_lane == slot - 1)
-    at_north = inside & (wide_lane == slot + 3)
-    for j in range(2):
-        south_at, north_at = (255, 128) if j == 0 else (127, 0)
-        picked = jnp.where(at_south, press[:, south_at : south_at + 1], 0.0) + jnp.where(
-            at_north, press[:, north_at : north_at + 1], 0.0
-        )
-        total = jnp.sum(picked.reshape(groups, 8, 128), axis=1, keepdims=True)
-        total = jnp.broadcast_to(total, (groups, 8, 128)).reshape(tall_rows, 128)
-        press_out[j * tall_rows : (j + 1) * tall_rows, :] = jnp.where(
-            slot == 6, total, press[:, j * 128 : j * 128 + 128]
-        )
+    press_out[0:half_rows, :] = press[:, 0:128]
+    press_out[half_rows : 2 * half_rows, :] = press[:, 128:256]
     exchange(
         1,
         press_out,
         press_in,
-        16,
-        lambda i, j: j * tall_rows + i * 16,
-        lambda i, j: (i * 2 + j) * 16,
+        8,
+        lambda i, j: j * half_rows + i * 8,
+        lambda i, j: (i * 2 + j) * 8,
     )
     back = halves(back_ref[...])
-    arrive(1, press_out, press_in, 16)
+    arrive(1, press_out, press_in, 8)
     modal_press = jnp.concatenate(
-        [press_in[pl.ds(s, 64, stride=8), :] for s in range(7)], axis=1
+        [press_in[pl.ds(x, 64, stride=4), :] for x in range(4)], axis=1
     )
     full = product(back, halves(modal_press))
-    at = [full[:, s * 128 : s * 128 + 128] for s in range(7)]
-    for x in range(4):
-        out_ref[pl.ds(x, 64, stride=4), :] = keep[x, 0] - 0.5 * (at[x + 2] - at[x])
-        out_ref[pl.ds(256 + x, 64, stride=4), :] = keep[x, 1] - dy(
-            at[x + 1], column(at[6], x), column(at[6], 4 + x)
-        )
-        out_ref[pl.ds(512 + x, 64, stride=4), :] = keep[x, 2] - dz(at[x + 1])
+    at = [full[:, x * 128 : x * 128 + 128] for x in range(4)]
+
+    def swap(n, source, target, to_east, to_north):
+        return pltpu.make_async_remote_copy(
+            src_ref=source,
+            dst_ref=target,
+            send_sem=plane_send.at[n],
+            recv_sem=plane_recv.at[n],
+            device_id=(to_east, to_north),
+            device_id_type=MESH,
+        )
+
+    planes[0:64, :] = at[0]
+    planes[64:128, :] = at[3]
+    swaps = [
+        swap(0, planes.at[64:128], sides.at[0:64], right, gj),
+        swap(1, planes.at[0:64], sides.at[64:128], left, gj),
+        swap(2, strip, strip_in, gi, other),
+    ]
+    swaps[0].start()
+    swaps[1].start()
+    rim = jnp.zeros((64, 128), F32)
+    for x in range(4):
+        rim = jnp.where(lane // 4 == x, pltpu.roll(at[x], 4 * x + 2, 1), rim)
+    strip[...] = jnp.concatenate([rim, jnp.zeros((64, 128), F32)], axis=0).T[0:16]
+    swaps[2].start()
+
+    for x in range(4):
+        ahead = at[x + 1] if x < 3 else 0.0
+        behind = at[x - 1] if x > 0 else 0.0
+        out_ref[pl.ds(x, 64, stride=4), :] = keep[x, 0] - 0.5 * (ahead - behind)
+    stores[0].start()
+    for x in range(4):
+        out_ref[pl.ds(256 + x, 64, stride=4), :] = keep[x, 1] - dy(at[x], 0.0, 0.0)
+    stores[1].start()
+    for x in range(4):
+        out_ref[pl.ds(512 + x, 64, stride=4), :] = keep[x, 2] - dz(at[x])
+    stores[2].start()
+    for store in stores:
+        store.wait()
+    for copy in swaps:
+        copy.wait()
+
+
+def finish_kernel(result, sides, strip_in, out, fields, planes, strip, load_sem, side_sem, save_sem):
+    loads = [
+        pltpu.make_async_copy(
+            result.at[f * 256 : f * 256 + 256], fields.at[f * 256 : f * 256 + 256], load_sem.at[f]
+        )
+        for f in range(4)
+    ]
+    saves = [
+        pltpu.make_async_copy(
+            fields.at[f * 256 : f * 256 + 256], out.at[f * 256 : f * 256 + 256], save_sem.at[f]
+        )
+        for f in range(4)
+    ]
+    extra = [
+        pltpu.make_async_copy(strip_in, strip, side_sem.at[0]),
+        pltpu.make_async_copy(sides, planes, side_sem.at[1]),
+    ]
+    for copy in extra + loads:
+        copy.start()
+    extra[0].wait()
+    rim = jnp.concatenate([strip[...], jnp.zeros((112, 128), F32)], axis=0).T[0:64]
+    lane = lax.broadcasted_iota(jnp.int32, (64, 128), 1)
+    extra[1].wait()
+    loads[0].wait()
+    first, last = pl.ds(0, 64, stride=4), pl.ds(3, 64, stride=4)
+    fields[first, :] = fields[first, :] + 0.5 * planes[0:64]
+    fields[last, :] = fields[last, :] - 0.5 * planes[64:128]
+    saves[0].start()
+    loads[1].wait()
+    for x in range(4):
+        rows = pl.ds(256 + x, 64, stride=4)
+        south = 0.5 * pltpu.roll(rim, 127 - 4 * x, 1)
+        north = 0.5 * pltpu.roll(rim, 125 - 4 * x, 1)
+        fields[rows, :] = fields[rows, :] + (
+            jnp.where(lane == 0, south, 0.0) - jnp.where(lane == 127, north, 0.0)
+        )
+    saves[1].start()
+    for f in (3, 2):
+        loads[f].wait()
+        saves[f].start()
+    for save in saves:
+        save.wait()
 
 
 def in_one_kernel(
@@ -616,11 +692,16 @@
     def held(*extent):
         return pltpu.VMEM(extent, F32)
 
-    out = pl.pallas_call(
+    in_hbm = pl.BlockSpec(memory_space=pltpu.HBM)
+
+    def full_size(*extent):
+        return jax.ShapeDtypeStruct(extent, F32)
+
+    parts = pl.pallas_call(
         functools.partial(step_kernel, count_east),
-        out_shape=jax.ShapeDtypeStruct((1024, 128), F32),
-        in_specs=[pl.BlockSpec(memory_space=pltpu.HBM)] * len(operands),
-        out_specs=pl.BlockSpec(memory_space=pltpu.VMEM),
+        out_shape=(full_size(1024, 128), full_size(128, 128), full_size(16, 128)),
+        in_specs=[in_hbm] * len(operands),
+        out_specs=(in_hbm,) * 3,
         scratch_shapes=[pltpu.VMEM(operand.shape, operand.dtype) for operand in operands]
         + [
             pltpu.SemaphoreType.DMA((len(operands),)),
@@ -637,18 +718,39 @@
             held(32, 256),
             held(8 * devices, 128),
             held(8 * devices, 128),
-            held(16 * devices, 128),
-            held(16 * devices, 128),
+            held(8 * devices, 128),
+            held(8 * devices, 128),
             held(4, 4, 64, 128),
+            held(1024, 128),
+            held(128, 128),
+            held(16, 128),
+            pltpu.SemaphoreType.DMA((4,)),
             pltpu.SemaphoreType.DMA((9,)),
             pltpu.SemaphoreType.DMA((9,)),
             pltpu.SemaphoreType.DMA((2,)),
             pltpu.SemaphoreType.DMA((2,)),
+            pltpu.SemaphoreType.DMA((3,)),
+            pltpu.SemaphoreType.DMA((3,)),
         ],
         compiler_params=pltpu.CompilerParams(
             collective_id=0, has_side_effects=True, vmem_limit_bytes=63 * 1024 * 1024
         ),
     )(*operands)
+    out = pl.pallas_call(
+        finish_kernel,
+        out_shape=full_size(1024, 128),
+        in_specs=[in_hbm] * 3,
+        out_specs=in_hbm,
+        scratch_shapes=[
+            held(1024, 128),
+            held(128, 128),
+            held(16, 128),
+            pltpu.SemaphoreType.DMA((4,)),
+            pltpu.SemaphoreType.DMA((2,)),
+            pltpu.SemaphoreType.DMA((4,)),
+        ],
+        compiler_params=pltpu.CompilerParams(vmem_limit_bytes=63 * 1024 * 1024),
+    )(*parts)
     return out.reshape(shape)
 
 

time: 31.1 us -> 31.2 us (level)
  Pallas kernels: 29 us -> 31 us
  local copies, waits for them, and re-layouts: 1.87 us -> 0 us
    pallas_call x1 -> x2, Pallas kernels: 29 us -> 31 us  [the longest x1 29 us: in_one_kernel(): pl.pallas_call(functools.partial(step_kernel, count_east), out_shape=(ful...]
    unnamed x1 -> x0, local copies, waits for them, and re-layouts: 1.87 us -> none
where the time goes in v3:
time: 31.2 us; the launch traced here: 31.1 us
  Pallas kernels  31 us (99%)
    pallas_call x1, Pallas kernels, in_one_kernel(): pl.pallas_call(functools.partial(step_kernel, count_east), out_shape=(ful...  29 us
    pallas_call x1, Pallas kernels, in_one_kernel(): pl.pallas_call(finish_kernel, out_shape=full_size(1024, 128), in_specs=[i...  2.03 us

profile of v3, /device:TPU:0, one launch (start us, length us, event | category | flops | bytes accessed | tf_op | source)
XLA Modules:
  0.0 31.1 jit_solution(5189252224770875137)
XLA Ops:
  0.0 29.0 %shard_map.100 = (f32[1024,128]{1,0:T(8,128)}, f32[128,128]{1,0:T(8,128)}, f32[16,128]{1,0:T(8,128)}) custom-call(f32[1024,128]{1,0:T(8,128)} %bitcast.5, bf16[256,256]{1,0:T(8,128)(2,1)} %refs_1_.1, f32[1,256]{1,0:T(1,128)} %bitcast.6, bf16[256,128]{1,0:T(8,128)(2,1)} %refs_3_.1, f32[1,64]{1,0:T(1,128)} %bitcast.7, f32[1,64]{1,0:T(1,128)} %bitcast.8, ...), custom_call_target="tpu_custom_call" | custom-call | tf_op jit(solution)/shard_map/pallas_call | solution.py:700
  29.0 2.0 %shard_map.101 = f32[1024,128]{1,0:T(8,128)} custom-call(f32[1024,128]{1,0:T(8,128)} %get-tuple-element.8.result, f32[128,128]{1,0:T(8,128)} %get-tuple-element.9.sides, f32[16,128]{1,0:T(8,128)} %get-tuple-element.10.strip_in), custom_call_target="tpu_custom_call" | custom-call | tf_op jit(solution)/shard_map/pallas_call | solution.py:739

commit v4 on v2

--- a/solution.py
+++ b/solution.py
@@ -257,12 +257,12 @@
     basis_north, symbol_north = real_basis(total_north)
     blocks = total_east // cells_east
     gather = np.zeros((2, total_east, blocks, 2, cells_east))
-    spread = np.zeros((blocks, 2, 8, 2, total_east))
+    spread = np.zeros((blocks, 8, 2, 2, total_east))
     for mode in range(2):
         gather[mode, :, :, mode, :] = basis_east.T.reshape(total_east, blocks, cells_east)
         for slot in range(cells_east + 2):
             columns = (np.arange(blocks) * cells_east + slot - 1) % total_east
-            spread[:, mode, slot, mode, :] = basis_east[columns]
+            spread[:, slot, mode, mode, :] = basis_east[columns]
     symbol = symbol_east[:, None] + symbol_north[None, :]
     return (
         np.concatenate(
@@ -281,19 +281,19 @@
     count_east,
     *refs,
 ):
-    operands, out_ref, held = refs[:10], refs[10], refs[11:21]
-    step_body(count_east, operands, held, out_ref, *refs[21:])
+    operands, result, held = refs[:10], refs[10], refs[11:21]
+    step_body(count_east, operands, held, result, *refs[21:])
 
 
 def step_body(
     count_east,
     operands,
     held,
+    result,
+    fetch_sem,
+    slab_sem,
+    store_sem,
     out_ref,
-    fetch_sem,
-    own_u,
-    own_vw,
-    own_th,
     left_u,
     left_vw,
     left_th,
@@ -331,11 +331,17 @@
         table_ref,
         back_ref,
     ) = held
-    fetches = [
-        pltpu.make_async_copy(source, target, fetch_sem.at[n])
-        for n, (source, target) in enumerate(zip(operands, held))
+    state_in = operands[0]
+    slab_fetches = [
+        pltpu.make_async_copy(
+            state_in.at[pl.ds(0, 256), x], state_ref.at[x * 256 : x * 256 + 256], slab_sem.at[x]
+        )
+        for x in range(4)
     ]
-    for fetch in fetches:
+    fetches = {
+        n: pltpu.make_async_copy(operands[n], held[n], fetch_sem.at[n]) for n in range(1, 10)
+    }
+    for fetch in slab_fetches + list(fetches.values()):
         fetch.start()
     barrier = pltpu.get_barrier_semaphore()
 
@@ -350,16 +356,6 @@
     lane = lax.broadcasted_iota(jnp.int32, (64, 128), 1)
     level = lax.broadcasted_iota(jnp.int32, (64, 128), 0)
     lane_tall = lax.broadcasted_iota(jnp.int32, (256, 128), 1)
-
-    fetches[0].wait()
-    slabs = [state_ref[pl.ds(x, 256, stride=4), :] for x in range(4)]
-    edges = jnp.zeros((256, 128), F32)
-    for x in range(4):
-        own_u[x * 64 : x * 64 + 64, :] = slabs[x][0:64]
-        own_vw[x * 128 : x * 128 + 128, :] = slabs[x][64:192]
-        own_th[x * 64 : x * 64 + 64, :] = slabs[x][192:256]
-        edges = jnp.where(lane_tall // 4 == x, pltpu.roll(slabs[x], 4 * x + 2, 1), edges)
-    edge_out[...] = edges.T[0:16]
 
     pl.semaphore_wait(barrier, devices - 1)
 
@@ -373,19 +369,33 @@
             device_id_type=MESH,
         )
 
+    def plane(start, height, x):
+        return state_in.at[pl.ds(start, height), x]
+
     copies = [
-        halo(0, edge_out, edge_in.at[8:24], gi, other),
-        halo(1, edge_out.at[8:16], edge_in.at[0:8], right, other),
-        halo(2, edge_out.at[0:8], edge_in.at[24:32], left, other),
-        halo(3, own_u.at[128:256], left_u, right, gj),
-        halo(4, own_u.at[0:128], right_u, left, gj),
-        halo(5, own_vw.at[384:512], left_vw, right, gj),
-        halo(6, own_vw.at[0:128], right_vw, left, gj),
-        halo(7, own_th.at[192:256], left_th, right, gj),
-        halo(8, own_th.at[0:64], right_th, left, gj),
+        halo(0, plane(0, 64, 3), left_u.at[64:128], right, gj),
+        halo(1, plane(0, 64, 0), right_u.at[0:64], left, gj),
+        halo(2, plane(64, 128, 3), left_vw, right, gj),
+        halo(3, plane(64, 128, 0), right_vw, left, gj),
+        halo(4, plane(0, 64, 2), left_u.at[0:64], right, gj),
+        halo(5, plane(0, 64, 1), right_u.at[64:128], left, gj),
+        halo(6, edge_out, edge_in.at[8:24], gi, other),
+        halo(7, edge_out.at[8:16], edge_in.at[0:8], right, other),
+        halo(8, edge_out.at[0:8], edge_in.at[24:32], left, other),
+        halo(9, plane(192, 64, 3), left_th, right, gj),
+        halo(10, plane(192, 64, 0), right_th, left, gj),
     ]
-    for copy in copies:
+    for copy in copies[:6]:
         copy.start()
+    edges = jnp.zeros((256, 128), F32)
+    for x in range(4):
+        slab_fetches[x].wait()
+        rolled = pltpu.roll(state_ref[x * 256 : x * 256 + 256, :], 4 * x + 2, 1)
+        edges = jnp.where(lane_tall // 4 == x, rolled, edges)
+    edge_out[...] = edges.T[0:16]
+    for copy in copies[6:]:
+        copy.start()
+    slabs = [state_ref[x * 256 : x * 256 + 256, :] for x in range(4)]
 
     for n in range(1, 7):
         fetches[n].wait()
@@ -402,8 +412,8 @@
     inverse_density = 1.0 / density
     modes = lax.broadcasted_iota(jnp.int32, (1, 64), 1)
     rates = rate_ref[...]
-    rate_low = jnp.sum(jnp.where(modes == 2 * me, rates, 0.0), axis=1, keepdims=True)
-    rate_high = jnp.sum(jnp.where(modes == 2 * me + 1, rates, 0.0), axis=1, keepdims=True)
+    rate_low = jnp.sum(jnp.where(modes == me, rates, 0.0), axis=1, keepdims=True)
+    rate_high = jnp.sum(jnp.where(modes == me + devices, rates, 0.0), axis=1, keepdims=True)
     symbol = jnp.concatenate([symbol_ref[0:128], symbol_ref[128:256]], axis=1)
     tall = lax.broadcasted_iota(jnp.int32, (128, 256), 0)
     green = -1.0 / (jnp.where(tall < 64, rate_low, rate_high) + symbol)
@@ -418,18 +428,40 @@
         behind = jnp.where(lane == 0, south, pltpu.roll(values, 1, 1))
         return 0.5 * (ahead - behind)
 
-    def column(values, c):
-        return jnp.broadcast_to(values[:, c : c + 1], (64, 128))
-
-    for n in range(7):
+    def shift(values, by):
+        return pltpu.roll(values, by % 128, 1)
+
+    def beside(cols, x):
+        return shift(cols, -9 - 4 * x), shift(cols, 117 - 4 * x)
+
+    u = {x: slabs[x][0:64] for x in range(4)}
+    v = {x: slabs[x][64:128] for x in range(4)}
+    w = {x: slabs[x][128:192] for x in range(4)}
+    th = {x: slabs[x][192:256] for x in range(4)}
+
+    for x in range(4):
+        heat = forcing[0:64, x * 128 : x * 128 + 128]
+        lift = forcing[64:128, x * 128 : x * 128 + 128]
+        for f, values in enumerate((u, v, w, th)):
+            ahead = values[x + 1] if x < 3 else 0.0
+            behind = values[x - 1] if x > 0 else 0.0
+            change = -(
+                u[x] * (0.5 * (ahead - behind))
+                + v[x] * dy(values[x], 0.0, 0.0)
+                + w[x] * dz(values[x])
+            )
+            if f == 2:
+                change = change + (BUOYANCY * th[x] + lift)
+            if f == 3:
+                change = change + heat
+            keep[x, f] = values[x] + TIME_STEP * change
+
+    for n in range(9):
         copies[n].wait()
 
     halo_cols = jnp.concatenate([edge_in[...], jnp.zeros((96, 256), F32)], axis=0).T
     halo_u, halo_v, halo_w, halo_th = [halo_cols[f * 64 : f * 64 + 64] for f in range(4)]
     own_edges_v = edges[64:128]
-
-    def shift(values, by):
-        return pltpu.roll(values, by % 128, 1)
 
     is_south = lane % 4 == 1
     ahead = jnp.where(is_south, shift(own_edges_v, 7), shift(halo_v, -1))
@@ -440,48 +472,55 @@
         + halo_w * dz(halo_v)
     )
 
-    u = {x: slabs[x][0:64] for x in range(4)}
-    v = {x: slabs[x][64:128] for x in range(4)}
-    w = {x: slabs[x][128:192] for x in range(4)}
-    th = {x: slabs[x][192:256] for x in range(4)}
     u[-2], u[-1] = left_u[0:64], left_u[64:128]
     u[4], u[5] = right_u[0:64], right_u[64:128]
     v[-1], w[-1] = left_vw[0:64], left_vw[64:128]
     v[4], w[4] = right_vw[0:64], right_vw[64:128]
 
-    def tendency(f, cols, x):
-        south, north = column(cols, 9 + 4 * x), column(cols, 10 + 4 * x)
-        return -(
-            u[x] * (0.5 * (f[x + 1] - f[x - 1])) + v[x] * dy(f[x], south, north) + w[x] * dz(f[x])
-        )
-
-    east_star = {x: u[x] + TIME_STEP * tendency(u, halo_u, x) for x in range(-1, 5)}
+    def complete(f, values, cols, x):
+        south, north = beside(cols, x)
+        share = v[x] * (jnp.where(lane == 127, north, 0.0) - jnp.where(lane == 0, south, 0.0))
+        if x == 0:
+            share = share - u[x] * values[-1]
+        if x == 3:
+            share = share + u[x] * values[4]
+        return keep[x, f] - (0.5 * TIME_STEP) * share
+
+    def outer_u(x):
+        south, north = beside(halo_u, x)
+        return u[x] - TIME_STEP * (
+            u[x] * (0.5 * (u[x + 1] - u[x - 1])) + v[x] * dy(u[x], south, north) + w[x] * dz(u[x])
+        )
+
+    east_star = {x: outer_u(x) for x in (-1, 4)}
+    for x in range(4):
+        east_star[x] = complete(0, u, halo_u, x)
+        keep[x, 0] = east_star[x]
     pieces = []
     for x in range(4):
-        north_star = v[x] + TIME_STEP * tendency(v, halo_v, x)
-        heat = forcing[0:64, x * 128 : x * 128 + 128]
-        lift = forcing[64:128, x * 128 : x * 128 + 128]
-        up_star = w[x] + TIME_STEP * (tendency(w, halo_w, x) + BUOYANCY * th[x] + lift)
-        keep[x, 0] = east_star[x]
+        north_star = complete(1, v, halo_v, x)
+        up_star = complete(2, w, halo_w, x)
         keep[x, 1] = north_star
         keep[x, 2] = up_star
-        keep[x, 3] = heat
         pieces.append(
             0.5 * (east_star[x + 1] - east_star[x - 1])
-            + dy(north_star, column(outside_v, 9 + 4 * x), column(outside_v, 10 + 4 * x))
+            + dy(north_star, *beside(outside_v, x))
             + dz(density * up_star) * inverse_density
         )
     fetches[7].wait()
     modal = product(halves(forward_ref[...]), halves(jnp.concatenate(pieces, axis=1)))
     for x in range(4):
-        modal_out[pl.ds(x, 64, stride=4), :] = modal[:, x * 128 : x * 128 + 128]
-
-    def exchange(n, source, target, rows, from_place, to_place):
+        for mode in range(2):
+            modal_out[pl.ds(4 * mode + x, devices, stride=8), :] = modal[
+                mode * devices : (mode + 1) * devices, x * 128 : x * 128 + 128
+            ]
+
+    def exchange(n, source, target, rows, step, from_place, to_place):
         def landing(i, j):
-            return pl.ds(pl.multiple_of(to_place(i, j), rows), rows)
+            return pl.ds(pl.multiple_of(to_place(i, j), step), rows)
 
         def leaving(i, j):
-            return pl.ds(pl.multiple_of(from_place(i, j), rows), rows)
+            return pl.ds(pl.multiple_of(from_place(i, j), step), rows)
 
         for entry in partners:
             to = partner(*entry)
@@ -512,17 +551,25 @@
         modal_out,
         modal_in,
         8,
+        8,
         lambda i, j: (i * 2 + j) * 8,
         lambda i, j: j * half_rows + i * 8,
     )
 
-    for n in range(7, 9):
+    for n in range(9, 11):
         copies[n].wait()
     th[-1], th[4] = left_th[...], right_th[...]
-    for x in range(4):
-        out_ref[pl.ds(768 + x, 64, stride=4), :] = th[x] + TIME_STEP * (
-            tendency(th, halo_th, x) + keep[x, 3]
-        )
+    stores = [
+        pltpu.make_async_copy(
+            out_ref.at[f * 256 : f * 256 + 256],
+            result.at[f * 256 : f * 256 + 256],
+            store_sem.at[f],
+        )
+        for f in range(4)
+    ]
+    for x in range(4):
+        out_ref[pl.ds(768 + x, 64, stride=4), :] = complete(3, th, halo_th, x)
+    stores[3].start()
 
     for n in range(8, 10):
         fetches[n].wait()
@@ -547,43 +594,70 @@
     spread = product(spread_out, halves(spectral))
     press = product(halves(spread), north_back)
     tall_rows = 16 * count_east
-    groups = tall_rows // 8
-    slot = lax.broadcasted_iota(jnp.int32, (tall_rows, 128), 0) % 8
+    place = lax.broadcasted_iota(jnp.int32, (tall_rows, 128), 0) % 16
+    slot, mode = place // 2, place % 2
     wide_lane = lax.broadcasted_iota(jnp.int32, (tall_rows, 128), 1)
     inside = (slot >= 1) & (slot <= 4)
-    at_south = inside & (wide_lane == slot - 1)
-    at_north = inside & (wide_lane == slot + 3)
+    at_south = inside & (wide_lane == 8 * mode + slot - 1)
+    at_north = inside & (wide_lane == 8 * mode + slot + 3)
     for j in range(2):
         south_at, north_at = (255, 128) if j == 0 else (127, 0)
         picked = jnp.where(at_south, press[:, south_at : south_at + 1], 0.0) + jnp.where(
             at_north, press[:, north_at : north_at + 1], 0.0
         )
-        total = jnp.sum(picked.reshape(groups, 8, 128), axis=1, keepdims=True)
-        total = jnp.broadcast_to(total, (groups, 8, 128)).reshape(tall_rows, 128)
+        total = jnp.sum(picked.reshape(count_east, 16, 128), axis=1, keepdims=True)
+        total = jnp.broadcast_to(total, (count_east, 16, 128)).reshape(tall_rows, 128)
         press_out[j * tall_rows : (j + 1) * tall_rows, :] = jnp.where(
-            slot == 6, total, press[:, j * 128 : j * 128 + 128]
+            place == 12, total, press[:, j * 128 : j * 128 + 128]
         )
     exchange(
         1,
         press_out,
         press_in,
+        13,
         16,
         lambda i, j: j * tall_rows + i * 16,
         lambda i, j: (i * 2 + j) * 16,
     )
     back = halves(back_ref[...])
-    arrive(1, press_out, press_in, 16)
-    modal_press = jnp.concatenate(
-        [press_in[pl.ds(s, 64, stride=8), :] for s in range(7)], axis=1
-    )
+    arrive(1, press_out, press_in, 13)
+
+    def of_slot(s):
+        return jnp.concatenate(
+            [press_in[pl.ds(2 * s + mode, devices, stride=16), :] for mode in range(2)], axis=0
+        )
+
+    rim = press_in[pl.ds(12, devices, stride=16), :]
+    rim = jnp.concatenate([rim, shift(rim, -8)], axis=0)
+    modal_press = jnp.concatenate([of_slot(s) for s in range(6)] + [rim], axis=1)
     full = product(back, halves(modal_press))
     at = [full[:, s * 128 : s * 128 + 128] for s in range(7)]
     for x in range(4):
         out_ref[pl.ds(x, 64, stride=4), :] = keep[x, 0] - 0.5 * (at[x + 2] - at[x])
+    stores[0].start()
+    for x in range(4):
         out_ref[pl.ds(256 + x, 64, stride=4), :] = keep[x, 1] - dy(
-            at[x + 1], column(at[6], x), column(at[6], 4 + x)
-        )
+            at[x + 1], shift(at[6], -x), shift(at[6], 123 - x)
+        )
+    stores[1].start()
+    for x in range(4):
         out_ref[pl.ds(512 + x, 64, stride=4), :] = keep[x, 2] - dz(at[x + 1])
+    stores[2].start()
+    for store in stores:
+        store.wait()
+
+
+def hand_on_kernel(result, out, sem):
+    copies = [
+        pltpu.make_async_copy(
+            result.at[n * 128 : n * 128 + 128], out.at[n * 128 : n * 128 + 128], sem.at[n]
+        )
+        for n in range(8)
+    ]
+    for copy in copies:
+        copy.start()
+    for copy in copies:
+        copy.wait()
 
 
 def in_one_kernel(
@@ -601,7 +675,7 @@
     devices = 2 * count_east
     table, symbol = constant_tables(shape[2] * count_east, shape[3] * 2, shape[2])
     operands = (
-        model_state.reshape(1024, 128),
+        model_state.reshape(256, 4, 128),
         layer_in,
         layer_bias.reshape(1, -1),
         layer_out,
@@ -616,17 +690,20 @@
     def held(*extent):
         return pltpu.VMEM(extent, F32)
 
+    in_hbm = pl.BlockSpec(memory_space=pltpu.HBM)
+    full_size = jax.ShapeDtypeStruct((1024, 128), F32)
     out = pl.pallas_call(
         functools.partial(step_kernel, count_east),
-        out_shape=jax.ShapeDtypeStruct((1024, 128), F32),
-        in_specs=[pl.BlockSpec(memory_space=pltpu.HBM)] * len(operands),
-        out_specs=pl.BlockSpec(memory_space=pltpu.VMEM),
-        scratch_shapes=[pltpu.VMEM(operand.shape, operand.dtype) for operand in operands]
+        out_shape=full_size,
+        in_specs=[in_hbm] * len(operands),
+        out_specs=in_hbm,
+        scratch_shapes=[held(1024, 128)]
+        + [pltpu.VMEM(operand.shape, operand.dtype) for operand in operands[1:]]
         + [
             pltpu.SemaphoreType.DMA((len(operands),)),
-            held(256, 128),
-            held(512, 128),
-            held(256, 128),
+            pltpu.SemaphoreType.DMA((4,)),
+            pltpu.SemaphoreType.DMA((4,)),
+            held(1024, 128),
             held(128, 128),
             held(128, 128),
             held(64, 128),
@@ -640,8 +717,8 @@
             held(16 * devices, 128),
             held(16 * devices, 128),
             held(4, 4, 64, 128),
-            pltpu.SemaphoreType.DMA((9,)),
-            pltpu.SemaphoreType.DMA((9,)),
+            pltpu.SemaphoreType.DMA((11,)),
+            pltpu.SemaphoreType.DMA((11,)),
             pltpu.SemaphoreType.DMA((2,)),
             pltpu.SemaphoreType.DMA((2,)),
         ],
@@ -649,6 +726,14 @@
             collective_id=0, has_side_effects=True, vmem_limit_bytes=63 * 1024 * 1024
         ),
     )(*operands)
+    out = pl.pallas_call(
+        hand_on_kernel,
+        out_shape=full_size,
+        in_specs=[in_hbm],
+        out_specs=in_hbm,
+        scratch_shapes=[pltpu.SemaphoreType.DMA((8,))],
+        compiler_params=pltpu.CompilerParams(vmem_limit_bytes=63 * 1024 * 1024),
+    )(out)
     return out.reshape(shape)
 
 

time: 31.1 us -> 45.4 us (1.46)
  Pallas kernels: 29 us -> 45.2 us
  local copies, waits for them, and re-layouts: 1.87 us -> 0 us
    pallas_call x1 -> x2, Pallas kernels: 29 us -> 45.2 us  [the longest x1 28.2 us: in_one_kernel(): pl.pallas_call(functools.partial(step_kernel, count_east), out_shape=full...]
    unnamed x1 -> x0, local copies, waits for them, and re-layouts: 1.87 us -> none
where the time goes in v4:
time: 45.4 us; the launch traced here: 45.2 us
  Pallas kernels  45.2 us (100%)
    pallas_call x1, Pallas kernels, in_one_kernel(): pl.pallas_call(functools.partial(step_kernel, count_east), out_shape=full...  28.2 us
    pallas_call x1, Pallas kernels, in_one_kernel(): pl.pallas_call(hand_on_kernel, out_shape=full_size, in_specs=[in_hbm], ou...  17.1 us

profile of v4, /device:TPU:0, one launch (start us, length us, event | category | flops | bytes accessed | tf_op | source)
XLA Modules:
  0.0 45.2 jit_solution(8978308057708761726)
XLA Ops:
  0.0 28.2 %shard_map.100.result = f32[1024,128]{1,0:T(8,128)} custom-call(f32[256,4,128]{2,1,0:T(4,128)} %bitcast.5, bf16[256,256]{1,0:T(8,128)(2,1)} %refs_1_.1, f32[1,256]{1,0:T(1,128)} %bitcast.6, bf16[256,128]{1,0:T(8,128)(2,1)} %refs_3_.1, f32[1,64]{1,0:T(1,128)} %bitcast.7, f32[1,64]{1,0:T(1,128)} %bitcast.8, f32[256,128]{1,0:T(8,128)} %constant.4.clone.refs_6_, ...), custom_call_target="tpu_custom_call" | custom-call | tf_op jit(solution)/shard_map/pallas_call | solution.py:695
  28.2 17.1 %shard_map.101 = f32[1024,128]{1,0:T(8,128)} custom-call(f32[1024,128]{1,0:T(8,128)} %shard_map.100.result), custom_call_target="tpu_custom_call" | custom-call | tf_op jit(solution)/shard_map/pallas_call | solution.py:729

commit v5 on v4

--- a/solution.py
+++ b/solution.py
@@ -281,19 +281,18 @@
     count_east,
     *refs,
 ):
-    operands, result, held = refs[:10], refs[10], refs[11:21]
-    step_body(count_east, operands, held, result, *refs[21:])
+    operands, outs, held = refs[:9], refs[9:11], refs[11:20]
+    step_body(count_east, operands, held, outs, *refs[20:])
 
 
 def step_body(
     count_east,
     operands,
     held,
-    result,
+    outs,
     fetch_sem,
     slab_sem,
     store_sem,
-    out_ref,
     left_u,
     left_vw,
     left_th,
@@ -305,7 +304,6 @@
     modal_out,
     modal_in,
     press_out,
-    press_in,
     keep,
     halo_send,
     halo_recv,
@@ -329,8 +327,8 @@
         symbol_ref,
         forward_ref,
         table_ref,
-        back_ref,
     ) = held
+    stars, press_in = outs
     state_in = operands[0]
     slab_fetches = [
         pltpu.make_async_copy(
@@ -339,7 +337,7 @@
         for x in range(4)
     ]
     fetches = {
-        n: pltpu.make_async_copy(operands[n], held[n], fetch_sem.at[n]) for n in range(1, 10)
+        n: pltpu.make_async_copy(operands[n], held[n], fetch_sem.at[n]) for n in range(1, 9)
     }
     for fetch in slab_fetches + list(fetches.values()):
         fetch.start()
@@ -532,7 +530,11 @@
                 device_id=to,
                 device_id_type=MESH,
             ).start()
-        target[landing(gi, gj), :] = source[leaving(gi, gj), :]
+        own = pltpu.make_async_copy(
+            source.at[leaving(gi, gj)], target.at[landing(gi, gj)], store_sem.at[1 + n]
+        )
+        own.start()
+        return own
 
     def arrive(n, source, target, rows):
         total = (devices - 1) * rows
@@ -546,7 +548,7 @@
         ).wait()
 
     half_rows = 8 * count_east
-    exchange(
+    own = exchange(
         0,
         modal_out,
         modal_in,
@@ -559,19 +561,12 @@
     for n in range(9, 11):
         copies[n].wait()
     th[-1], th[4] = left_th[...], right_th[...]
-    stores = [
-        pltpu.make_async_copy(
-            out_ref.at[f * 256 : f * 256 + 256],
-            result.at[f * 256 : f * 256 + 256],
-            store_sem.at[f],
-        )
-        for f in range(4)
-    ]
-    for x in range(4):
-        out_ref[pl.ds(768 + x, 64, stride=4), :] = complete(3, th, halo_th, x)
-    stores[3].start()
-
-    for n in range(8, 10):
+    for x in range(4):
+        keep[x, 3] = complete(3, th, halo_th, x)
+    store = pltpu.make_async_copy(keep, stars, store_sem.at[0])
+    store.start()
+
+    for n in range(8, 9):
         fetches[n].wait()
     wide = 2 * half_rows
 
@@ -586,6 +581,7 @@
     gather = table(4 * wide, half_rows, 1)
     spread_out = table(5 * wide, wide, 1)
     north_back = table(7 * wide, wide, 2)
+    own.wait()
     arrive(0, modal_out, modal_in, 8)
 
     rows = jnp.concatenate([modal_in[0:half_rows], modal_in[half_rows : 2 * half_rows]], axis=1)
@@ -610,7 +606,7 @@
         press_out[j * tall_rows : (j + 1) * tall_rows, :] = jnp.where(
             place == 12, total, press[:, j * 128 : j * 128 + 128]
         )
-    exchange(
+    own = exchange(
         1,
         press_out,
         press_in,
@@ -619,45 +615,73 @@
         lambda i, j: j * tall_rows + i * 16,
         lambda i, j: (i * 2 + j) * 16,
     )
-    back = halves(back_ref[...])
+    own.wait()
+    store.wait()
     arrive(1, press_out, press_in, 13)
+
+
+def last_kernel(
+    devices, stars, press_in, back_ref, out, held, press, back_held, fields, load_sem, save_sem
+):
+    loads = [
+        pltpu.make_async_copy(back_ref, back_held, load_sem.at[0]),
+        pltpu.make_async_copy(press_in, press, load_sem.at[1]),
+    ] + [pltpu.make_async_copy(stars.at[x], held.at[x], load_sem.at[2 + x]) for x in range(4)]
+    saves = [
+        pltpu.make_async_copy(
+            fields.at[f * 256 : f * 256 + 256], out.at[f * 256 : f * 256 + 256], save_sem.at[f]
+        )
+        for f in range(4)
+    ]
+    for load in loads:
+        load.start()
+    lane = lax.broadcasted_iota(jnp.int32, (64, 128), 1)
+    level = lax.broadcasted_iota(jnp.int32, (64, 128), 0)
+
+    def shift(values, by):
+        return pltpu.roll(values, by % 128, 1)
+
+    def dz(values):
+        up = jnp.where(level == 63, 0.0, pltpu.roll(values, 63, 0))
+        down = jnp.where(level == 0, 0.0, pltpu.roll(values, 1, 0))
+        return 0.5 * (up - down)
+
+    def dy(values, south, north):
+        ahead = jnp.where(lane == 127, north, shift(values, -1))
+        behind = jnp.where(lane == 0, south, shift(values, 1))
+        return 0.5 * (ahead - behind)
 
     def of_slot(s):
         return jnp.concatenate(
-            [press_in[pl.ds(2 * s + mode, devices, stride=16), :] for mode in range(2)], axis=0
-        )
-
-    rim = press_in[pl.ds(12, devices, stride=16), :]
+            [press[pl.ds(2 * s + mode, devices, stride=16), :] for mode in range(2)], axis=0
+        )
+
+    loads[0].wait()
+    back = halves(back_held[...])
+    loads[1].wait()
+    rim = press[pl.ds(12, devices, stride=16), :]
     rim = jnp.concatenate([rim, shift(rim, -8)], axis=0)
     modal_press = jnp.concatenate([of_slot(s) for s in range(6)] + [rim], axis=1)
     full = product(back, halves(modal_press))
     at = [full[:, s * 128 : s * 128 + 128] for s in range(7)]
-    for x in range(4):
-        out_ref[pl.ds(x, 64, stride=4), :] = keep[x, 0] - 0.5 * (at[x + 2] - at[x])
-    stores[0].start()
-    for x in range(4):
-        out_ref[pl.ds(256 + x, 64, stride=4), :] = keep[x, 1] - dy(
+    for load in loads[2:]:
+        load.wait()
+    for x in range(4):
+        fields[pl.ds(768 + x, 64, stride=4), :] = held[x, 3]
+    saves[3].start()
+    for x in range(4):
+        fields[pl.ds(x, 64, stride=4), :] = held[x, 0] - 0.5 * (at[x + 2] - at[x])
+    saves[0].start()
+    for x in range(4):
+        fields[pl.ds(256 + x, 64, stride=4), :] = held[x, 1] - dy(
             at[x + 1], shift(at[6], -x), shift(at[6], 123 - x)
         )
-    stores[1].start()
-    for x in range(4):
-        out_ref[pl.ds(512 + x, 64, stride=4), :] = keep[x, 2] - dz(at[x + 1])
-    stores[2].start()
-    for store in stores:
-        store.wait()
-
-
-def hand_on_kernel(result, out, sem):
-    copies = [
-        pltpu.make_async_copy(
-            result.at[n * 128 : n * 128 + 128], out.at[n * 128 : n * 128 + 128], sem.at[n]
-        )
-        for n in range(8)
-    ]
-    for copy in copies:
-        copy.start()
-    for copy in copies:
-        copy.wait()
+    saves[1].start()
+    for x in range(4):
+        fields[pl.ds(512 + x, 64, stride=4), :] = held[x, 2] - dz(at[x + 1])
+    saves[2].start()
+    for save in saves:
+        save.wait()
 
 
 def in_one_kernel(
@@ -684,26 +708,27 @@
         symbol,
         mode_forward,
         table,
-        mode_back,
     )
 
     def held(*extent):
         return pltpu.VMEM(extent, F32)
 
     in_hbm = pl.BlockSpec(memory_space=pltpu.HBM)
-    full_size = jax.ShapeDtypeStruct((1024, 128), F32)
-    out = pl.pallas_call(
+
+    def whole(*extent):
+        return jax.ShapeDtypeStruct(extent, F32)
+
+    parts = pl.pallas_call(
         functools.partial(step_kernel, count_east),
-        out_shape=full_size,
+        out_shape=(whole(4, 4, 64, 128), whole(16 * devices, 128)),
         in_specs=[in_hbm] * len(operands),
-        out_specs=in_hbm,
+        out_specs=(in_hbm, in_hbm),
         scratch_shapes=[held(1024, 128)]
         + [pltpu.VMEM(operand.shape, operand.dtype) for operand in operands[1:]]
         + [
             pltpu.SemaphoreType.DMA((len(operands),)),
             pltpu.SemaphoreType.DMA((4,)),
-            pltpu.SemaphoreType.DMA((4,)),
-            held(1024, 128),
+            pltpu.SemaphoreType.DMA((3,)),
             held(128, 128),
             held(128, 128),
             held(64, 128),
@@ -714,7 +739,6 @@
             held(32, 256),
             held(8 * devices, 128),
             held(8 * devices, 128),
-            held(16 * devices, 128),
             held(16 * devices, 128),
             held(4, 4, 64, 128),
             pltpu.SemaphoreType.DMA((11,)),
@@ -727,13 +751,20 @@
         ),
     )(*operands)
     out = pl.pallas_call(
-        hand_on_kernel,
-        out_shape=full_size,
-        in_specs=[in_hbm],
+        functools.partial(last_kernel, devices),
+        out_shape=whole(1024, 128),
+        in_specs=[in_hbm] * 3,
         out_specs=in_hbm,
-        scratch_shapes=[pltpu.SemaphoreType.DMA((8,))],
+        scratch_shapes=[
+            held(4, 4, 64, 128),
+            held(16 * devices, 128),
+            held(64, 64),
+            held(1024, 128),
+            pltpu.SemaphoreType.DMA((6,)),
+            pltpu.SemaphoreType.DMA((4,)),
+        ],
         compiler_params=pltpu.CompilerParams(vmem_limit_bytes=63 * 1024 * 1024),
-    )(out)
+    )(*parts, mode_back)
     return out.reshape(shape)
 
 

time: 45.4 us -> 29.5 us (0.65)
  Pallas kernels: 45.2 us -> 29.4 us
    pallas_call x2, Pallas kernels: 45.2 us -> 29.4 us  [the longest x1 27.1 us: in_one_kernel(): pl.pallas_call(functools.partial(step_kernel, count_east), out_shape=(who...]
where the time goes in v5:
time: 29.5 us; the launch traced here: 29.4 us
  Pallas kernels  29.4 us (100%)
    pallas_call x1, Pallas kernels, in_one_kernel(): pl.pallas_call(functools.partial(step_kernel, count_east), out_shape=(who...  27.1 us
    pallas_call x1, Pallas kernels, in_one_kernel(): pl.pallas_call(functools.partial(last_kernel, devices), out_shape=whole(1...  2.25 us

profile of v5, /device:TPU:0, one launch (start us, length us, event | category | flops | bytes accessed | tf_op | source)
XLA Modules:
  0.0 29.4 jit_solution(5797923164405063489)
XLA Ops:
  0.0 27.1 %shard_map.100 = (f32[4,4,64,128]{3,2,1,0:T(8,128)}, f32[512,128]{1,0:T(8,128)}) custom-call(f32[256,4,128]{2,1,0:T(4,128)} %bitcast.5, bf16[256,256]{1,0:T(8,128)(2,1)} %refs_1_.1, f32[1,256]{1,0:T(1,128)} %bitcast.6, bf16[256,128]{1,0:T(8,128)(2,1)} %refs_3_.1, f32[1,64]{1,0:T(1,128)} %bitcast.7, f32[1,64]{1,0:T(1,128)} %bitcast.8, ...), custom_call_target="tpu_custom_call" | custom-call | tf_op jit(solution)/shard_map/pallas_call | solution.py:721
  27.1 2.3 %shard_map.101 = f32[1024,128]{1,0:T(8,128)} custom-call(f32[4,4,64,128]{3,2,1,0:T(8,128)} %get-tuple-element.7.stars, f32[512,128]{1,0:T(8,128)} %get-tuple-element.8.press_in, f32[64,64]{1,0:T(8,128)} %back_ref.1), custom_call_target="tpu_custom_call" | custom-call | tf_op jit(solution)/shard_map/pallas_call | solution.py:753

commit v6 on v5

--- a/solution.py
+++ b/solution.py
@@ -293,6 +293,7 @@
     fetch_sem,
     slab_sem,
     store_sem,
+    own,
     left_u,
     left_vw,
     left_th,
@@ -332,9 +333,9 @@
     state_in = operands[0]
     slab_fetches = [
         pltpu.make_async_copy(
-            state_in.at[pl.ds(0, 256), x], state_ref.at[x * 256 : x * 256 + 256], slab_sem.at[x]
-        )
-        for x in range(4)
+            state_in.at[f * 256 : f * 256 + 256], state_ref.at[f * 256 : f * 256 + 256], slab_sem.at[f]
+        )
+        for f in range(4)
     ]
     fetches = {
         n: pltpu.make_async_copy(operands[n], held[n], fetch_sem.at[n]) for n in range(1, 9)
@@ -355,6 +356,12 @@
     level = lax.broadcasted_iota(jnp.int32, (64, 128), 0)
     lane_tall = lax.broadcasted_iota(jnp.int32, (256, 128), 1)
 
+    for f in range(4):
+        slab_fetches[f].wait()
+        for x in (3, 0, 2, 1):
+            own[x * 256 + f * 64 : x * 256 + f * 64 + 64, :] = state_ref[
+                pl.ds(f * 256 + x, 64, stride=4), :
+            ]
     pl.semaphore_wait(barrier, devices - 1)
 
     def halo(n, source, target, to_east, to_north):
@@ -368,7 +375,7 @@
         )
 
     def plane(start, height, x):
-        return state_in.at[pl.ds(start, height), x]
+        return own.at[x * 256 + start : x * 256 + start + height]
 
     copies = [
         halo(0, plane(0, 64, 3), left_u.at[64:128], right, gj),
@@ -387,13 +394,12 @@
         copy.start()
     edges = jnp.zeros((256, 128), F32)
     for x in range(4):
-        slab_fetches[x].wait()
-        rolled = pltpu.roll(state_ref[x * 256 : x * 256 + 256, :], 4 * x + 2, 1)
+        rolled = pltpu.roll(own[x * 256 : x * 256 + 256, :], 4 * x + 2, 1)
         edges = jnp.where(lane_tall // 4 == x, rolled, edges)
     edge_out[...] = edges.T[0:16]
     for copy in copies[6:]:
         copy.start()
-    slabs = [state_ref[x * 256 : x * 256 + 256, :] for x in range(4)]
+    slabs = [own[x * 256 : x * 256 + 256, :] for x in range(4)]
 
     for n in range(1, 7):
         fetches[n].wait()
@@ -530,11 +536,11 @@
                 device_id=to,
                 device_id_type=MESH,
             ).start()
-        own = pltpu.make_async_copy(
+        mine = pltpu.make_async_copy(
             source.at[leaving(gi, gj)], target.at[landing(gi, gj)], store_sem.at[1 + n]
         )
-        own.start()
-        return own
+        mine.start()
+        return mine
 
     def arrive(n, source, target, rows):
         total = (devices - 1) * rows
@@ -548,7 +554,7 @@
         ).wait()
 
     half_rows = 8 * count_east
-    own = exchange(
+    mine = exchange(
         0,
         modal_out,
         modal_in,
@@ -581,7 +587,7 @@
     gather = table(4 * wide, half_rows, 1)
     spread_out = table(5 * wide, wide, 1)
     north_back = table(7 * wide, wide, 2)
-    own.wait()
+    mine.wait()
     arrive(0, modal_out, modal_in, 8)
 
     rows = jnp.concatenate([modal_in[0:half_rows], modal_in[half_rows : 2 * half_rows]], axis=1)
@@ -606,7 +612,7 @@
         press_out[j * tall_rows : (j + 1) * tall_rows, :] = jnp.where(
             place == 12, total, press[:, j * 128 : j * 128 + 128]
         )
-    own = exchange(
+    mine = exchange(
         1,
         press_out,
         press_in,
@@ -615,7 +621,7 @@
         lambda i, j: j * tall_rows + i * 16,
         lambda i, j: (i * 2 + j) * 16,
     )
-    own.wait()
+    mine.wait()
     store.wait()
     arrive(1, press_out, press_in, 13)
 
@@ -699,7 +705,7 @@
     devices = 2 * count_east
     table, symbol = constant_tables(shape[2] * count_east, shape[3] * 2, shape[2])
     operands = (
-        model_state.reshape(256, 4, 128),
+        model_state.reshape(1024, 128),
         layer_in,
         layer_bias.reshape(1, -1),
         layer_out,
@@ -729,6 +735,7 @@
             pltpu.SemaphoreType.DMA((len(operands),)),
             pltpu.SemaphoreType.DMA((4,)),
             pltpu.SemaphoreType.DMA((3,)),
+            held(1024, 128),
             held(128, 128),
             held(128, 128),
             held(64, 128),

time: 29.5 us -> 29.3 us (level)
  no operation moved by 1% of the time
where the time goes in v6:
time: 29.3 us; the launch traced here: 29.2 us
  Pallas kernels  29.2 us (100%)
    pallas_call x1, Pallas kernels, in_one_kernel(): pl.pallas_call(functools.partial(step_kernel, count_east), out_shape=(who...  26.9 us
    pallas_call x1, Pallas kernels, in_one_kernel(): pl.pallas_call(functools.partial(last_kernel, devices), out_shape=whole(1...  2.25 us

profile of v6, /device:TPU:0, one launch (start us, length us, event | category | flops | bytes accessed | tf_op | source)
XLA Modules:
  0.0 29.2 jit_solution(12795481618973612427)
XLA Ops:
  0.0 26.9 %shard_map.100 = (f32[4,4,64,128]{3,2,1,0:T(8,128)}, f32[512,128]{1,0:T(8,128)}) custom-call(f32[1024,128]{1,0:T(8,128)} %bitcast.5, bf16[256,256]{1,0:T(8,128)(2,1)} %refs_1_.1, f32[1,256]{1,0:T(1,128)} %bitcast.6, bf16[256,128]{1,0:T(8,128)(2,1)} %refs_3_.1, f32[1,64]{1,0:T(1,128)} %bitcast.7, f32[1,64]{1,0:T(1,128)} %bitcast.8, ...), custom_call_target="tpu_custom_call" | custom-call | tf_op jit(solution)/shard_map/pallas_call | solution.py:727
  26.9 2.3 %shard_map.101 = f32[1024,128]{1,0:T(8,128)} custom-call(f32[4,4,64,128]{3,2,1,0:T(8,128)} %get-tuple-element.7.stars, f32[512,128]{1,0:T(8,128)} %get-tuple-element.8.press_in, f32[64,64]{1,0:T(8,128)} %back_ref.1), custom_call_target="tpu_custom_call" | custom-call | tf_op jit(solution)/shard_map/pallas_call | solution.py:760

commit v7 on v6

--- a/solution.py
+++ b/solution.py
@@ -269,7 +269,7 @@
             [
                 pair(basis_north),
                 pair(gather.reshape(2 * total_east, -1)),
-                pair(spread.reshape(-1, 2 * total_east)),
+                pair(np.concatenate([spread, spread]).reshape(-1, 2 * total_east)),
                 pair(basis_north.T),
             ]
         ),
@@ -414,14 +414,6 @@
         jnp.concatenate([density_ref[...], jnp.ones((1, 64), F32)], axis=1), (128, 128)
     ).T[0:64]
     inverse_density = 1.0 / density
-    modes = lax.broadcasted_iota(jnp.int32, (1, 64), 1)
-    rates = rate_ref[...]
-    rate_low = jnp.sum(jnp.where(modes == me, rates, 0.0), axis=1, keepdims=True)
-    rate_high = jnp.sum(jnp.where(modes == me + devices, rates, 0.0), axis=1, keepdims=True)
-    symbol = jnp.concatenate([symbol_ref[0:128], symbol_ref[128:256]], axis=1)
-    tall = lax.broadcasted_iota(jnp.int32, (128, 256), 0)
-    green = -1.0 / (jnp.where(tall < 64, rate_low, rate_high) + symbol)
-
     def dz(values):
         up = jnp.where(level == 63, 0.0, pltpu.roll(values, 63, 0))
         down = jnp.where(level == 0, 0.0, pltpu.roll(values, 1, 0))
@@ -444,9 +436,8 @@
     th = {x: slabs[x][192:256] for x in range(4)}
 
     for x in range(4):
-        heat = forcing[0:64, x * 128 : x * 128 + 128]
         lift = forcing[64:128, x * 128 : x * 128 + 128]
-        for f, values in enumerate((u, v, w, th)):
+        for f, values in enumerate((u, v, w)):
             ahead = values[x + 1] if x < 3 else 0.0
             behind = values[x - 1] if x > 0 else 0.0
             change = -(
@@ -456,8 +447,6 @@
             )
             if f == 2:
                 change = change + (BUOYANCY * th[x] + lift)
-            if f == 3:
-                change = change + heat
             keep[x, f] = values[x] + TIME_STEP * change
 
     for n in range(9):
@@ -519,28 +508,18 @@
                 mode * devices : (mode + 1) * devices, x * 128 : x * 128 + 128
             ]
 
-    def exchange(n, source, target, rows, step, from_place, to_place):
-        def landing(i, j):
-            return pl.ds(pl.multiple_of(to_place(i, j), step), rows)
-
-        def leaving(i, j):
-            return pl.ds(pl.multiple_of(from_place(i, j), step), rows)
-
-        for entry in partners:
-            to = partner(*entry)
-            pltpu.make_async_remote_copy(
-                src_ref=source.at[leaving(*to)],
-                dst_ref=target.at[landing(gi, gj)],
-                send_sem=swap_send.at[n],
-                recv_sem=swap_recv.at[n],
-                device_id=to,
-                device_id_type=MESH,
-            ).start()
-        mine = pltpu.make_async_copy(
-            source.at[leaving(gi, gj)], target.at[landing(gi, gj)], store_sem.at[1 + n]
-        )
-        mine.start()
-        return mine
+    def send(n, source, target, to):
+        return pltpu.make_async_remote_copy(
+            src_ref=source,
+            dst_ref=target,
+            send_sem=swap_send.at[n],
+            recv_sem=swap_recv.at[n],
+            device_id=to,
+            device_id_type=MESH,
+        )
+
+    def tile(start, step, rows):
+        return pl.ds(pl.multiple_of(start, step), rows)
 
     def arrive(n, source, target, rows):
         total = (devices - 1) * rows
@@ -554,16 +533,20 @@
         ).wait()
 
     half_rows = 8 * count_east
-    mine = exchange(
-        0,
-        modal_out,
-        modal_in,
-        8,
-        8,
-        lambda i, j: (i * 2 + j) * 8,
-        lambda i, j: j * half_rows + i * 8,
-    )
-
+    landing = modal_in.at[tile(gj * half_rows + gi * 8, 8, 8)]
+    for entry in partners:
+        to = partner(*entry)
+        send(0, modal_out.at[tile((to[0] * 2 + to[1]) * 8, 8, 8)], landing, to).start()
+    mine = pltpu.make_async_copy(modal_out.at[tile(me * 8, 8, 8)], landing, store_sem.at[1])
+    mine.start()
+
+    for x in range(4):
+        ahead = th[x + 1] if x < 3 else 0.0
+        behind = th[x - 1] if x > 0 else 0.0
+        keep[x, 3] = th[x] + TIME_STEP * (
+            forcing[0:64, x * 128 : x * 128 + 128]
+            - (u[x] * (0.5 * (ahead - behind)) + v[x] * dy(th[x], 0.0, 0.0) + w[x] * dz(th[x]))
+        )
     for n in range(9, 11):
         copies[n].wait()
     th[-1], th[4] = left_th[...], right_th[...]
@@ -574,6 +557,13 @@
 
     for n in range(8, 9):
         fetches[n].wait()
+    modes = lax.broadcasted_iota(jnp.int32, (1, 64), 1)
+    rates = rate_ref[...]
+    rate_low = jnp.sum(jnp.where(modes == me, rates, 0.0), axis=1, keepdims=True)
+    rate_high = jnp.sum(jnp.where(modes == me + devices, rates, 0.0), axis=1, keepdims=True)
+    symbol = jnp.concatenate([symbol_ref[0:128], symbol_ref[128:256]], axis=1)
+    tall = lax.broadcasted_iota(jnp.int32, (128, 256), 0)
+    green = -1.0 / (jnp.where(tall < 64, rate_low, rate_high) + symbol)
     wide = 2 * half_rows
 
     def table(start, height, width):
@@ -585,42 +575,55 @@
 
     north = table(0, wide, 2)
     gather = table(4 * wide, half_rows, 1)
-    spread_out = table(5 * wide, wide, 1)
-    north_back = table(7 * wide, wide, 2)
+    north_back = table(9 * wide, wide, 2)
     mine.wait()
     arrive(0, modal_out, modal_in, 8)
 
     rows = jnp.concatenate([modal_in[0:half_rows], modal_in[half_rows : 2 * half_rows]], axis=1)
     spectral = product(halves(rows), north)
     spectral = product(gather, halves(spectral)) * green
-    spread = product(spread_out, halves(spectral))
-    press = product(halves(spread), north_back)
-    tall_rows = 16 * count_east
-    place = lax.broadcasted_iota(jnp.int32, (tall_rows, 128), 0) % 16
+    spectral = halves(spectral)
+    turn = count_east // 4
+    begin = lax.rem(gi + turn, count_east) * 16
+    place = lax.broadcasted_iota(jnp.int32, (half_rows, 128), 0) % 16
     slot, mode = place // 2, place % 2
-    wide_lane = lax.broadcasted_iota(jnp.int32, (tall_rows, 128), 1)
+    wide_lane = lax.broadcasted_iota(jnp.int32, (half_rows, 128), 1)
     inside = (slot >= 1) & (slot <= 4)
     at_south = inside & (wide_lane == 8 * mode + slot - 1)
     at_north = inside & (wide_lane == 8 * mode + slot + 3)
-    for j in range(2):
-        south_at, north_at = (255, 128) if j == 0 else (127, 0)
-        picked = jnp.where(at_south, press[:, south_at : south_at + 1], 0.0) + jnp.where(
-            at_north, press[:, north_at : north_at + 1], 0.0
-        )
-        total = jnp.sum(picked.reshape(count_east, 16, 128), axis=1, keepdims=True)
-        total = jnp.broadcast_to(total, (count_east, 16, 128)).reshape(tall_rows, 128)
-        press_out[j * tall_rows : (j + 1) * tall_rows, :] = jnp.where(
-            place == 12, total, press[:, j * 128 : j * 128 + 128]
-        )
-    mine = exchange(
-        1,
-        press_out,
-        press_in,
-        13,
-        16,
-        lambda i, j: j * tall_rows + i * 16,
-        lambda i, j: (i * 2 + j) * 16,
-    )
+    landing = press_in.at[tile(me * 16, 16, 13)]
+    count = count_east // 2
+    for half in range(2):
+        rows_at = begin + 5 * wide + half * half_rows
+        spread = product(
+            (
+                table_ref[tile(rows_at, 16, half_rows), :],
+                table_ref[tile(rows_at + 2 * wide, 16, half_rows), :],
+            ),
+            spectral,
+        )
+        press = product(halves(spread), north_back)
+        for j in range(2):
+            south_at, north_at = (255, 128) if j == 0 else (127, 0)
+            picked = jnp.where(at_south, press[:, south_at : south_at + 1], 0.0) + jnp.where(
+                at_north, press[:, north_at : north_at + 1], 0.0
+            )
+            total = jnp.sum(picked.reshape(count, 16, 128), axis=1, keepdims=True)
+            total = jnp.broadcast_to(total, (count, 16, 128)).reshape(half_rows, 128)
+            first_row = j * wide + half * half_rows
+            press_out[first_row : first_row + half_rows, :] = jnp.where(
+                place == 12, total, press[:, j * 128 : j * 128 + 128]
+            )
+        for q in sorted(range(count), key=lambda q: abs(2 * q - count + 1)):
+            steps = (turn + half * count + q) % count_east
+            for across in range(2):
+                to = partner(steps, across)
+                source = press_out.at[tile(to[1] * wide + half * half_rows + q * 16, 16, 13)]
+                if steps or across:
+                    send(1, source, landing, to).start()
+                else:
+                    mine = pltpu.make_async_copy(source, landing, store_sem.at[2])
+                    mine.start()
     mine.wait()
     store.wait()
     arrive(1, press_out, press_in, 13)

time: 29.3 us -> 28.8 us (0.983)
  Pallas kernels: 29.2 us -> 28.7 us
    pallas_call x1, Pallas kernels: 26.9 us -> 26.4 us  [in_one_kernel(): pl.pallas_call(functools.partial(step_kernel, count_east), out_shape=(who...]
where the time goes in v7:
time: 28.8 us; the launch traced here: 28.7 us
  Pallas kernels  28.7 us (100%)
    pallas_call x1, Pallas kernels, in_one_kernel(): pl.pallas_call(functools.partial(step_kernel, count_east), out_shape=(who...  26.4 us
    pallas_call x1, Pallas kernels, in_one_kernel(): pl.pallas_call(functools.partial(last_kernel, devices), out_shape=whole(1...  2.25 us

profile of v7, /device:TPU:0, one launch (start us, length us, event | category | flops | bytes accessed | tf_op | source)
XLA Modules:
  0.0 28.7 jit_solution(17249187116969623911)
XLA Ops:
  0.0 26.4 %shard_map.100 = (f32[4,4,64,128]{3,2,1,0:T(8,128)}, f32[512,128]{1,0:T(8,128)}) custom-call(f32[1024,128]{1,0:T(8,128)} %bitcast.5, bf16[256,256]{1,0:T(8,128)(2,1)} %refs_1_.1, f32[1,256]{1,0:T(1,128)} %bitcast.6, bf16[256,128]{1,0:T(8,128)(2,1)} %refs_3_.1, f32[1,64]{1,0:T(1,128)} %bitcast.7, f32[1,64]{1,0:T(1,128)} %bitcast.8, ...), custom_call_target="tpu_custom_call" | custom-call | tf_op jit(solution)/shard_map/pallas_call | solution.py:730
  26.4 2.3 %shard_map.101 = f32[1024,128]{1,0:T(8,128)} custom-call(f32[4,4,64,128]{3,2,1,0:T(8,128)} %get-tuple-element.7.stars, f32[512,128]{1,0:T(8,128)} %get-tuple-element.8.press_in, f32[64,64]{1,0:T(8,128)} %back_ref.1), custom_call_target="tpu_custom_call" | custom-call | tf_op jit(solution)/shard_map/pallas_call | solution.py:763

commit v8 on v7

--- a/solution.py
+++ b/solution.py
@@ -449,8 +449,8 @@
                 change = change + (BUOYANCY * th[x] + lift)
             keep[x, f] = values[x] + TIME_STEP * change
 
-    for n in range(9):
-        copies[n].wait()
+    for n in range(6, 9):
+        copies[n].wait_recv()
 
     halo_cols = jnp.concatenate([edge_in[...], jnp.zeros((96, 256), F32)], axis=0).T
     halo_u, halo_v, halo_w, halo_th = [halo_cols[f * 64 : f * 64 + 64] for f in range(4)]
@@ -465,6 +465,8 @@
         + halo_w * dz(halo_v)
     )
 
+    for n in range(6):
+        copies[n].wait_recv()
     u[-2], u[-1] = left_u[0:64], left_u[64:128]
     u[4], u[5] = right_u[0:64], right_u[64:128]
     v[-1], w[-1] = left_vw[0:64], left_vw[64:128]
@@ -521,16 +523,16 @@
     def tile(start, step, rows):
         return pl.ds(pl.multiple_of(start, step), rows)
 
-    def arrive(n, source, target, rows):
+    def arrived(n, source, target, rows):
         total = (devices - 1) * rows
-        pltpu.make_async_remote_copy(
+        return pltpu.make_async_remote_copy(
             src_ref=source.at[0:total],
             dst_ref=target.at[0:total],
             send_sem=swap_send.at[n],
             recv_sem=swap_recv.at[n],
             device_id=(right, gj),
             device_id_type=MESH,
-        ).wait()
+        )
 
     half_rows = 8 * count_east
     landing = modal_in.at[tile(gj * half_rows + gi * 8, 8, 8)]
@@ -548,7 +550,7 @@
             - (u[x] * (0.5 * (ahead - behind)) + v[x] * dy(th[x], 0.0, 0.0) + w[x] * dz(th[x]))
         )
     for n in range(9, 11):
-        copies[n].wait()
+        copies[n].wait_recv()
     th[-1], th[4] = left_th[...], right_th[...]
     for x in range(4):
         keep[x, 3] = complete(3, th, halo_th, x)
@@ -577,7 +579,8 @@
     gather = table(4 * wide, half_rows, 1)
     north_back = table(9 * wide, wide, 2)
     mine.wait()
-    arrive(0, modal_out, modal_in, 8)
+    forward = arrived(0, modal_out, modal_in, 8)
+    forward.wait_recv()
 
     rows = jnp.concatenate([modal_in[0:half_rows], modal_in[half_rows : 2 * half_rows]], axis=1)
     spectral = product(halves(rows), north)
@@ -626,7 +629,10 @@
                     mine.start()
     mine.wait()
     store.wait()
-    arrive(1, press_out, press_in, 13)
+    backward = arrived(1, press_out, press_in, 13)
+    for copy in copies + [forward, backward]:
+        copy.wait_send()
+    backward.wait_recv()
 
 
 def last_kernel(

time: 28.8 us -> 28.9 us (level)
  no operation moved by 1% of the time
where the time goes in v8:
time: 28.9 us; the launch traced here: 28.8 us
  Pallas kernels  28.8 us (100%)
    pallas_call x1, Pallas kernels, in_one_kernel(): pl.pallas_call(functools.partial(step_kernel, count_east), out_shape=(who...  26.5 us
    pallas_call x1, Pallas kernels, in_one_kernel(): pl.pallas_call(functools.partial(last_kernel, devices), out_shape=whole(1...  2.25 us

profile of v8, /device:TPU:0, one launch (start us, length us, event | category | flops | bytes accessed | tf_op | source)
XLA Modules:
  0.0 28.8 jit_solution(11217122357437237888)
XLA Ops:
  0.0 26.5 %shard_map.100 = (f32[4,4,64,128]{3,2,1,0:T(8,128)}, f32[512,128]{1,0:T(8,128)}) custom-call(f32[1024,128]{1,0:T(8,128)} %bitcast.5, bf16[256,256]{1,0:T(8,128)(2,1)} %refs_1_.1, f32[1,256]{1,0:T(1,128)} %bitcast.6, bf16[256,128]{1,0:T(8,128)(2,1)} %refs_3_.1, f32[1,64]{1,0:T(1,128)} %bitcast.7, f32[1,64]{1,0:T(1,128)} %bitcast.8, ...), custom_call_target="tpu_custom_call" | custom-call | tf_op jit(solution)/shard_map/pallas_call | solution.py:736
  26.5 2.3 %shard_map.101 = f32[1024,128]{1,0:T(8,128)} custom-call(f32[4,4,64,128]{3,2,1,0:T(8,128)} %get-tuple-element.7.stars, f32[512,128]{1,0:T(8,128)} %get-tuple-element.8.press_in, f32[64,64]{1,0:T(8,128)} %back_ref.1), custom_call_target="tpu_custom_call" | custom-call | tf_op jit(solution)/shard_map/pallas_call | solution.py:769

commit v9 on v7

--- a/solution.py
+++ b/solution.py
@@ -665,6 +665,11 @@
             [press[pl.ds(2 * s + mode, devices, stride=16), :] for mode in range(2)], axis=0
         )
 
+    for load in loads[2:]:
+        load.wait()
+    for x in range(4):
+        fields[pl.ds(768 + x, 64, stride=4), :] = held[x, 3]
+    saves[3].start()
     loads[0].wait()
     back = halves(back_held[...])
     loads[1].wait()
@@ -673,11 +678,6 @@
     modal_press = jnp.concatenate([of_slot(s) for s in range(6)] + [rim], axis=1)
     full = product(back, halves(modal_press))
     at = [full[:, s * 128 : s * 128 + 128] for s in range(7)]
-    for load in loads[2:]:
-        load.wait()
-    for x in range(4):
-        fields[pl.ds(768 + x, 64, stride=4), :] = held[x, 3]
-    saves[3].start()
     for x in range(4):
         fields[pl.ds(x, 64, stride=4), :] = held[x, 0] - 0.5 * (at[x + 2] - at[x])
     saves[0].start()

time: 28.8 us -> 29 us (level)
  no operation moved by 1% of the time
where the time goes in v9:
time: 29 us; the launch traced here: 28.8 us
  Pallas kernels  28.8 us (99%)
    pallas_call x1, Pallas kernels, in_one_kernel(): pl.pallas_call(functools.partial(step_kernel, count_east), out_shape=(who...  26.4 us
    pallas_call x1, Pallas kernels, in_one_kernel(): pl.pallas_call(functools.partial(last_kernel, devices), out_shape=whole(1...  2.41 us

profile of v9, /device:TPU:0, one launch (start us, length us, event | category | flops | bytes accessed | tf_op | source)
XLA Modules:
  0.0 28.8 jit_solution(4337944796923552802)
XLA Ops:
  0.0 26.4 %shard_map.100 = (f32[4,4,64,128]{3,2,1,0:T(8,128)}, f32[512,128]{1,0:T(8,128)}) custom-call(f32[1024,128]{1,0:T(8,128)} %bitcast.5, bf16[256,256]{1,0:T(8,128)(2,1)} %refs_1_.1, f32[1,256]{1,0:T(1,128)} %bitcast.6, bf16[256,128]{1,0:T(8,128)(2,1)} %refs_3_.1, f32[1,64]{1,0:T(1,128)} %bitcast.7, f32[1,64]{1,0:T(1,128)} %bitcast.8, ...), custom_call_target="tpu_custom_call" | custom-call | tf_op jit(solution)/shard_map/pallas_call | solution.py:730
  26.4 2.4 %shard_map.101 = f32[1024,128]{1,0:T(8,128)} custom-call(f32[4,4,64,128]{3,2,1,0:T(8,128)} %get-tuple-element.7.stars, f32[512,128]{1,0:T(8,128)} %get-tuple-element.8.press_in, f32[64,64]{1,0:T(8,128)} %back_ref.1), custom_call_target="tpu_custom_call" | custom-call | tf_op jit(solution)/shard_map/pallas_call | solution.py:763
